TPU v7x, 32 devices: a whole 2x2x4 slice. The times are simulated.
32 devices in a mesh: dp: 8 (over z, y), stream: 4 (over x, core).
Axes of the slice: x: 2, y: 2, z: 4, core: 2. Of those that a mesh axis runs over, the one named last changes fastest.
Arguments:
- text_input: bfloat16 [2, 128, 40, 768], P(None, ('dp', 'stream')), may hold values from -6 to 6
- patch_input: bfloat16 [2, 32, 145, 1024], P(None, ('dp', 'stream')), may hold values from -6 to 6
- text_lengths: int32 [2, 128], P(None, ('dp', 'stream')), may hold values from 6 to 40, as said below
- image_of_row: int32 [2, 128], P(None, ('dp', 'stream')), may hold values from 0 to 3, as said below
- cotangent: bfloat16 [2, 128, 40, 768], P(None, ('dp', 'stream')), may hold values from -6 to 6
- self_qkv: bfloat16 [3, 768, 768], P(None, 'dp'), may hold values from -0.21875 to 0.21875
- self_out: bfloat16 [768, 768], P('dp'), may hold values from -0.4375 to 0.4375
- cross_q: bfloat16 [768, 768], P('dp'), may hold values from -0.21875 to 0.21875
- cross_kv: bfloat16 [2, 1024, 768], P(None, 'dp'), may hold values from -0.1875 to 0.1875
- cross_out: bfloat16 [768, 768], P('dp'), may hold values from -0.75 to 0.75
- ffn_in: bfloat16 [768, 3072], P('dp'), may hold values from -0.21875 to 0.21875
- ffn_out: bfloat16 [3072, 768], P('dp'), may hold values from -0.109375 to 0.109375
- biases: bfloat16 [10, 768], P(None, 'dp'), may hold values from -1 to 1
- norm_gains: bfloat16 [3, 768], P(None, 'dp'), may hold values from 0.25 to 1.75
- ffn_bias: bfloat16 [3072], P('dp'), may hold values from -1 to 1
Outputs:
- layer_out: bfloat16 [2, 128, 40, 768], P(None, ('dp', 'stream'))
- text_grad: bfloat16 [2, 128, 40, 768], P(None, ('dp', 'stream'))
- patch_grad: bfloat16 [2, 32, 145, 1024], P(None, ('dp', 'stream'))
- grad_self_qkv: float32 [3, 768, 768], P(None, 'dp')
- grad_self_out: float32 [768, 768], P('dp')
- grad_cross_q: float32 [768, 768], P('dp')
- grad_cross_kv: float32 [2, 1024, 768], P(None, 'dp')
- grad_cross_out: float32 [768, 768], P('dp')
- grad_ffn_in: float32 [768, 3072], P('dp')
- grad_ffn_out: float32 [3072, 768], P('dp')
- grad_biases: float32 [10, 768], P(None, 'dp')
- grad_norm_gains: float32 [3, 768], P(None, 'dp')
- grad_ffn_bias: float32 [3072], P('dp')
Inputs may be any that keep to these rules, and one draw needn't show every extreme that they name: `text_lengths`: valid tokens of each row, counted from the row's start. `image_of_row`: each row names one of the 4 images of its group.
All inputs are finite; a program needn't handle non-finite values.
Results may differ from a plain program's by a relative error of at most 0.02.
Values may be sent and summed in bfloat16 or wider, within the bound.
No kernel may reach another device: no remote copies, remote signals or barrier semaphores. Data moves between devices by JAX's collectives and lax.ppermute only.
A program may use at most 512 MiB of HBM per device.

v0:
```python
import math

import jax
import jax.numpy as jnp
from jax import lax
from jax.sharding import PartitionSpec as P

HEADS = 12


EPSILON = 1e-06
ROOT_HALF = 0.7071067811865476
INV_ROOT_TAU = 0.3989422804014327
HIGHEST = lax.Precision.HIGHEST


def product(left, right):
    return jnp.dot(left, right, preferred_element_type=jnp.float32)


def contract_rows(left, right):
    return lax.dot_general(
        left, right, (((0,), (0,)), ((), ())), preferred_element_type=jnp.float32
    )


def contract_last(left, right):
    return lax.dot_general(
        left, right, (((1,), (1,)), ((), ())), preferred_element_type=jnp.float32
    )


def column_sum(matrix):
    return jnp.sum(matrix.astype(jnp.float32), axis=0)


def norm_forward(summed, gain_row, shift_row):
    center = summed - jnp.mean(summed, axis=-1, keepdims=True)
    inverse = lax.rsqrt(jnp.mean(center * center, axis=-1, keepdims=True) + EPSILON)
    normed = center * inverse
    return (normed * gain_row + shift_row, normed, inverse)


def norm_backward(upstream, normed, inverse, gain_row):
    scaled = upstream * gain_row
    grad_input = inverse * (
        scaled
        - jnp.mean(scaled, axis=-1, keepdims=True)
        - normed * jnp.mean(scaled * normed, axis=-1, keepdims=True)
    )
    return (grad_input, jnp.sum(upstream * normed, axis=0), jnp.sum(upstream, axis=0))


def softmax_rows(scores):
    row_peak = jnp.max(scores, axis=-1, keepdims=True)
    raised = jnp.exp(scores - row_peak)
    return raised / jnp.sum(raised, axis=-1, keepdims=True)


def gelu_value(hidden_pre):
    return 0.5 * hidden_pre * (1.0 + lax.erf(hidden_pre * ROOT_HALF))


def gelu_slope(hidden_pre):
    return 0.5 * (1.0 + lax.erf(hidden_pre * ROOT_HALF)) + hidden_pre * INV_ROOT_TAU * jnp.exp(
        -0.5 * hidden_pre * hidden_pre
    )


def micro_batch(weights, word_rows, pixels, lengths, images, upstream_rows):
    (
        self_qkv,
        self_out,
        cross_q,
        cross_kv,
        cross_out,
        ffn_in,
        ffn_out,
        biases,
        norm_gains,
        ffn_bias,
    ) = weights
    bias_rows = biases.astype(jnp.float32)
    gain_rows = norm_gains.astype(jnp.float32)
    ffn_shift = ffn_bias.astype(jnp.float32)
    row_count, seq_len, width_all = word_rows.shape
    head_size = width_all // HEADS
    patch_count = pixels.shape[1]
    score_scale = 1.0 / math.sqrt(head_size)
    tokens = row_count * seq_len
    flat_tokens = word_rows.reshape(tokens, width_all)
    position = jnp.arange(tokens, dtype=jnp.int32)
    segment = position // seq_len
    key_ok = position % seq_len < jnp.repeat(lengths, seq_len, total_repeat_length=tokens)
    allowed = (segment[:, None] == segment[None, :]) & key_ok[None, :]
    projected = jnp.einsum("nd,jde->jne", flat_tokens, self_qkv, preferred_element_type=jnp.float32)
    queries = (projected[0] + bias_rows[0]).astype(jnp.bfloat16).reshape(tokens, HEADS, head_size)
    keys_self = projected[1].astype(jnp.bfloat16).reshape(tokens, HEADS, head_size)
    values_self = (
        (projected[2] + bias_rows[1]).astype(jnp.bfloat16).reshape(tokens, HEADS, head_size)
    )
    scores = (
        jnp.einsum("qhc,khc->hqk", queries, keys_self, preferred_element_type=jnp.float32)
        * score_scale
    )
    attention = softmax_rows(jnp.where(allowed[None], scores, -jnp.inf))
    attention_low = attention.astype(jnp.bfloat16)
    attended = (
        jnp.einsum("hqk,khc->qhc", attention_low, values_self, preferred_element_type=jnp.float32)
        .reshape(tokens, width_all)
        .astype(jnp.bfloat16)
    )
    branch = product(attended, self_out) + bias_rows[2]
    first_norm, first_normed, first_inverse = norm_forward(
        flat_tokens.astype(jnp.float32) + branch, gain_rows[0], bias_rows[3]
    )
    first_low = first_norm.astype(jnp.bfloat16)
    cross_query = (product(first_low, cross_q) + bias_rows[4]).astype(jnp.bfloat16)
    cross_query_heads = cross_query.reshape(row_count, seq_len, HEADS, head_size)
    image_kv = jnp.einsum("ipv,jvd->jipd", pixels, cross_kv, preferred_element_type=jnp.float32)
    own_kv = jnp.stack((image_kv[0], image_kv[1] + bias_rows[5])).astype(jnp.bfloat16)
    group_kv = lax.all_gather(own_kv, "stream", axis=1, tiled=True)
    group_count = group_kv.shape[1]
    row_kv = jnp.take(group_kv, images, axis=1)
    row_keys = row_kv[0].reshape(row_count, patch_count, HEADS, head_size)
    row_values = row_kv[1].reshape(row_count, patch_count, HEADS, head_size)
    cross_scores = (
        jnp.einsum(
            "rqhc,rkhc->rhqk", cross_query_heads, row_keys, preferred_element_type=jnp.float32
        )
        * score_scale
    )
    cross_attention = softmax_rows(cross_scores)
    cross_low = cross_attention.astype(jnp.bfloat16)
    cross_heads = (
        jnp.einsum("rhqk,rkhc->rqhc", cross_low, row_values, preferred_element_type=jnp.float32)
        .reshape(tokens, width_all)
        .astype(jnp.bfloat16)
    )
    cross_branch = product(cross_heads, cross_out) + bias_rows[6]
    second_norm, second_normed, second_inverse = norm_forward(
        first_norm + cross_branch, gain_rows[1], bias_rows[7]
    )
    second_low = second_norm.astype(jnp.bfloat16)
    hidden_pre = product(second_low, ffn_in) + ffn_shift
    active = gelu_value(hidden_pre).astype(jnp.bfloat16)
    lowered = product(active, ffn_out) + bias_rows[8]
    output_rows, third_normed, third_inverse = norm_forward(
        second_norm + lowered, gain_rows[2], bias_rows[9]
    )
    upstream = (
        upstream_rows.reshape(tokens, width_all).astype(jnp.float32)
        * key_ok.astype(jnp.float32)[:, None]
    )
    grad_third, third_gain, third_shift = norm_backward(
        upstream, third_normed, third_inverse, gain_rows[2]
    )
    grad_lowered = grad_third.astype(jnp.bfloat16)
    grad_ffn_out = contract_rows(active, grad_lowered)
    grad_hidden = (contract_last(grad_lowered, ffn_out) * gelu_slope(hidden_pre)).astype(
        jnp.bfloat16
    )
    grad_ffn_in = contract_rows(second_low, grad_hidden)
    grad_second_total = grad_third + contract_last(grad_hidden, ffn_in)
    grad_second, second_gain, second_shift = norm_backward(
        grad_second_total, second_normed, second_inverse, gain_rows[1]
    )
    grad_cross_branch = grad_second.astype(jnp.bfloat16)
    grad_cross_out = contract_rows(cross_heads, grad_cross_branch)
    grad_cross_heads = (
        contract_last(grad_cross_branch, cross_out)
        .astype(jnp.bfloat16)
        .reshape(row_count, seq_len, HEADS, head_size)
    )
    grad_cross_attention = jnp.einsum(
        "rqhc,rkhc->rhqk", grad_cross_heads, row_values, preferred_element_type=jnp.float32
    )
    grad_row_values = jnp.einsum(
        "rhqk,rqhc->rkhc", cross_low, grad_cross_heads, preferred_element_type=jnp.float32
    )
    grad_cross_scores = (
        cross_attention
        * (
            grad_cross_attention
            - jnp.sum(grad_cross_attention * cross_attention, axis=-1, keepdims=True)
        )
    ).astype(jnp.bfloat16)
    grad_cross_query = (
        (
            jnp.einsum(
                "rhqk,rkhc->rqhc", grad_cross_scores, row_keys, preferred_element_type=jnp.float32
            )
            * score_scale
        )
        .astype(jnp.bfloat16)
        .reshape(tokens, width_all)
    )
    grad_row_keys = (
        jnp.einsum(
            "rhqk,rqhc->rkhc",
            grad_cross_scores,
            cross_query_heads,
            preferred_element_type=jnp.float32,
        )
        * score_scale
    )
    grad_rows_kv = jnp.stack(
        (
            grad_row_keys.reshape(row_count, patch_count, width_all),
            grad_row_values.reshape(row_count, patch_count, width_all),
        )
    )
    selector = (images[:, None] == jnp.arange(group_count, dtype=jnp.int32)[None, :]).astype(
        jnp.float32
    )
    grad_group_kv = jnp.einsum("ri,jrpd->ijpd", selector, grad_rows_kv, precision=HIGHEST)
    grad_own_kv = lax.psum_scatter(
        grad_group_kv.astype(jnp.bfloat16), "stream", scatter_dimension=0, tiled=True
    )
    grad_cross_kv = jnp.einsum(
        "ipv,ijpd->vjd", pixels, grad_own_kv, preferred_element_type=jnp.float32
    )
    value_bias = jnp.sum(grad_own_kv[:, 1].astype(jnp.float32), axis=(0, 1))
    grad_pixels = jnp.einsum(
        "ijpd,jvd->ipv", grad_own_kv, cross_kv, preferred_element_type=jnp.float32
    ).astype(jnp.bfloat16)
    grad_cross_q = contract_rows(first_low, grad_cross_query)
    grad_first_total = grad_second + contract_last(grad_cross_query, cross_q)
    grad_first, first_gain, first_shift = norm_backward(
        grad_first_total, first_normed, first_inverse, gain_rows[0]
    )
    grad_branch = grad_first.astype(jnp.bfloat16)
    grad_self_out = contract_rows(attended, grad_branch)
    grad_attended = (
        contract_last(grad_branch, self_out).astype(jnp.bfloat16).reshape(tokens, HEADS, head_size)
    )
    grad_attention = jnp.einsum(
        "qhc,khc->hqk", grad_attended, values_self, preferred_element_type=jnp.float32
    )
    grad_values = jnp.einsum(
        "hqk,qhc->khc", attention_low, grad_attended, preferred_element_type=jnp.float32
    )
    grad_scores = (
        attention * (grad_attention - jnp.sum(grad_attention * attention, axis=-1, keepdims=True))
    ).astype(jnp.bfloat16)
    grad_queries = (
        jnp.einsum("hqk,khc->qhc", grad_scores, keys_self, preferred_element_type=jnp.float32)
        * score_scale
    )
    grad_keys = (
        jnp.einsum("hqk,qhc->khc", grad_scores, queries, preferred_element_type=jnp.float32)
        * score_scale
    )
    grad_qkv_low = (
        jnp.stack((grad_queries, grad_keys, grad_values))
        .astype(jnp.bfloat16)
        .reshape(3, tokens, width_all)
    )
    grad_self_qkv = jnp.einsum(
        "nd,jne->dje", flat_tokens, grad_qkv_low, preferred_element_type=jnp.float32
    )
    grad_text = grad_first + jnp.einsum(
        "jne,jde->nd", grad_qkv_low, self_qkv, preferred_element_type=jnp.float32
    )
    grad_biases = jnp.stack(
        (
            column_sum(grad_qkv_low[0]),
            column_sum(grad_qkv_low[2]),
            column_sum(grad_branch),
            first_shift,
            column_sum(grad_cross_query),
            value_bias,
            column_sum(grad_cross_branch),
            second_shift,
            column_sum(grad_lowered),
            third_shift,
        ),
        axis=1,
    )
    grad_gains = jnp.stack((first_gain, second_gain, third_gain), axis=1)
    grads = (
        grad_self_qkv,
        grad_self_out,
        grad_cross_q,
        grad_cross_kv,
        grad_cross_out,
        grad_ffn_in,
        grad_ffn_out,
        grad_biases,
        grad_gains,
        column_sum(grad_hidden),
    )
    return (
        output_rows.astype(jnp.bfloat16).reshape(row_count, seq_len, width_all),
        grad_text.astype(jnp.bfloat16).reshape(row_count, seq_len, width_all),
        grad_pixels,
        grads,
    )


def stream_total(shards):
    streams = lax.axis_size("stream")
    flat_parts = [piece.reshape(-1) for piece in shards]
    joined = jnp.concatenate(flat_parts)
    length = joined.shape[0]
    padded_len = -(-length // streams) * streams
    joined = jnp.pad(joined, (0, padded_len - length)).reshape(streams, padded_len // streams)
    own_share = lax.psum_scatter(
        joined.astype(jnp.bfloat16), "stream", scatter_dimension=0, tiled=True
    ).astype(jnp.float32)
    combined = (
        lax.all_gather(own_share.astype(jnp.bfloat16), "stream", axis=0, tiled=True)
        .astype(own_share.dtype)
        .reshape(-1)
    )
    results = []
    offset = 0
    for piece in shards:
        count = piece.size
        results.append(combined[offset : offset + count].reshape(piece.shape))
        offset = offset + count
    return results


def on_device(
    text_input,
    patch_input,
    text_lengths,
    image_of_row,
    cotangent,
    self_qkv,
    self_out,
    cross_q,
    cross_kv,
    cross_out,
    ffn_in,
    ffn_out,
    biases,
    norm_gains,
    ffn_bias,
):
    output_list = []
    text_list = []
    patch_list = []
    totals = None
    for micro_step in range(text_input.shape[0]):
        gathered = (
            lax.all_gather(self_qkv, "dp", axis=1, tiled=True),
            lax.all_gather(self_out, "dp", axis=0, tiled=True),
            lax.all_gather(cross_q, "dp", axis=0, tiled=True),
            lax.all_gather(cross_kv, "dp", axis=1, tiled=True),
            lax.all_gather(cross_out, "dp", axis=0, tiled=True),
            lax.all_gather(ffn_in, "dp", axis=0, tiled=True),
            lax.all_gather(ffn_out, "dp", axis=0, tiled=True),
            lax.all_gather(biases, "dp", axis=1, tiled=True),
            lax.all_gather(norm_gains, "dp", axis=1, tiled=True),
            lax.all_gather(ffn_bias, "dp", axis=0, tiled=True),
        )
        output_rows, text_rows, patch_rows, grads = micro_batch(
            gathered,
            text_input[micro_step],
            patch_input[micro_step],
            text_lengths[micro_step],
            image_of_row[micro_step],
            cotangent[micro_step],
        )
        output_list.append(output_rows)
        text_list.append(text_rows)
        patch_list.append(patch_rows)
        totals = (
            grads if totals is None else tuple((left + right for left, right in zip(totals, grads)))
        )
    totals = (
        lax.psum_scatter(totals[0], "dp", scatter_dimension=0, tiled=True),
        lax.psum_scatter(totals[1], "dp", scatter_dimension=0, tiled=True),
        lax.psum_scatter(totals[2], "dp", scatter_dimension=0, tiled=True),
        lax.psum_scatter(totals[3], "dp", scatter_dimension=0, tiled=True),
        lax.psum_scatter(totals[4], "dp", scatter_dimension=0, tiled=True),
        lax.psum_scatter(totals[5], "dp", scatter_dimension=0, tiled=True),
        lax.psum_scatter(totals[6], "dp", scatter_dimension=0, tiled=True),
        lax.psum_scatter(totals[7], "dp", scatter_dimension=0, tiled=True),
        lax.psum_scatter(totals[8], "dp", scatter_dimension=0, tiled=True),
        lax.psum_scatter(totals[9], "dp", scatter_dimension=0, tiled=True),
    )
    summed = stream_total(list(totals))
    grad_self_qkv = jnp.transpose(summed[0], (1, 0, 2))
    grad_cross_kv = jnp.transpose(summed[3], (1, 0, 2))
    grad_biases = jnp.transpose(summed[7])
    grad_gains = jnp.transpose(summed[8])
    return (
        jnp.stack(output_list),
        jnp.stack(text_list),
        jnp.stack(patch_list),
        grad_self_qkv,
        summed[1],
        summed[2],
        grad_cross_kv,
        summed[4],
        summed[5],
        summed[6],
        grad_biases,
        grad_gains,
        summed[9],
    )


def solution(mesh):
    placed = (
        P(None, ("dp", "stream"), None, None),
        P(None, ("dp", "stream"), None, None),
        P(None, ("dp", "stream")),
        P(None, ("dp", "stream")),
        P(None, ("dp", "stream"), None, None),
        P(None, "dp", None),
        P("dp", None),
        P("dp", None),
        P(None, "dp", None),
        P("dp", None),
        P("dp", None),
        P("dp", None),
        P(None, "dp"),
        P(None, "dp"),
        P("dp"),
    )
    return jax.shard_map(
        on_device,
        mesh=mesh,
        in_specs=placed,
        out_specs=(
            P(None, ("dp", "stream"), None, None),
            P(None, ("dp", "stream"), None, None),
            P(None, ("dp", "stream"), None, None),
            P(None, "dp", None),
            P("dp", None),
            P("dp", None),
            P(None, "dp", None),
            P("dp", None),
            P("dp", None),
            P("dp", None),
            P(None, "dp"),
            P(None, "dp"),
            P("dp"),
        ),
        check_vma=False,
    )
```

profile of v0, /device:TPU:1, one launch (start us, length us, event | category | flops | bytes accessed | tf_op | source)
XLA Modules:
  0.0 2126.9 jit_solution(1475754440817653035)
XLA Ops:
  10.0 25.6 %all-gather = bf16[8,96,10]{1,2,0:T(8,128)(2,1)S(1)} all-gather(bf16[1,96,10]{1,2,0:T(8,128)(2,1)} %bitcast.352), channel_id=1, replica_groups=mesh['dp'=8,'stream'=4] {'dp'}, dimensions={0}, use_global_device_ids=true | all-gather | bytes 17280 | tf_op jit(solution)/shard_map/all_gather | solution.py:355
  37.2 35.0 %all-gather.19.cloned.1.call-done = bf16[2,1024,768]{2,1,0:T(8,128)(2,1)} async-done(((bf16[2,128,768]{2,1,0:T(8,128)(2,1)}), bf16[2,1024,768]{2,1,0:T(8,128)(2,1)}) %all-gather.19.cloned.1.call-update) | async-done | bytes 3145744 | tf_op jit(solution)/shard_map/all_gather | solution.py:351
  82.4 5.2 fusion.176
  89.0 15.4 all-gather.1
  108.3 22.6 %all-gather.2 = bf16[8,1,384]{2,1,0:T(2,128)(2,1)S(1)} all-gather(bf16[1,1,384]{2,1,0:T(2,128)(2,1)S(1)} %reshape.779), channel_id=1, replica_groups=mesh['dp'=8,'stream'=4] {'dp'}, dimensions={0}, use_global_device_ids=true | all-gather | bytes 6912 | tf_op jit(solution)/shard_map/all_gather | solution.py:357
  132.6 5.7 all-gather.15.cloned.1.call-done
  138.3 2.9 convolution_bitcast_fusion
  152.7 27.2 %all-gather.17.cloned.1.call-done = bf16[768,768]{1,0:T(8,128)(2,1)} async-done(((bf16[96,768]{1,0:T(8,128)(2,1)}), bf16[768,768]{1,0:T(8,128)(2,1)}) %all-gather.17.cloned.1.call-update) | async-done | bytes 1179664 | tf_op jit(solution)/shard_map/all_gather | solution.py:349
  183.9 37.9 %all-gather.23.cloned.1.call-done = bf16[768,768]{1,0:T(8,128)(2,1)} async-done(((bf16[96,768]{1,0:T(8,128)(2,1)}), bf16[768,768]{1,0:T(8,128)(2,1)}) %all-gather.23.cloned.1.call-update) | async-done | bytes 1179664 | tf_op jit(solution)/shard_map/all_gather | solution.py:350
  230.6 14.4 all-gather.21.cloned.1.call-done
  245.0 6.9 gather_fusion
  251.9 15.3 all-gather.31.cloned.1.call-done
  267.3 7.4 gather_fusion.1
  274.7 5.2 fusion.22
  279.9 4.2 fusion.179
  284.1 5.0 copy.313
  289.1 5.0 copy.312
  298.1 5.5 fusion.42
  306.1 4.3 fusion.180
  310.4 3.7 copy.323
  314.1 5.4 copy.322
  322.9 5.5 fusion.43
  333.3 56.8 %all-gather.27.cloned.1.call-done = bf16[768,3072]{1,0:T(8,128)(2,1)} async-done(((bf16[96,3072]{1,0:T(8,128)(2,1)}), bf16[768,3072]{1,0:T(8,128)(2,1)}) %all-gather.27.cloned.1.call-update) | async-done | bytes 4718608 | tf_op jit(solution)/shard_map/all_gather | solution.py:353
  390.0 4.7 convolution_add_fusion.3
  394.8 75.5 %all-gather.29.cloned.1.call-done = bf16[3072,768]{1,0:T(8,128)(2,1)} async-done(((bf16[384,768]{1,0:T(8,128)(2,1)}), bf16[3072,768]{1,0:T(8,128)(2,1)}) %all-gather.29.cloned.1.call-update) | async-done | bytes 4718608 | tf_op jit(solution)/shard_map/all_gather | solution.py:354
  470.3 4.2 fusion.191
  498.2 7.0 fusion.66
  505.2 3.1 multiply_reduce_fusion.1
  511.7 7.0 fusion.71
  518.7 3.1 multiply_reduce_fusion.3
  535.9 2.9 convert_reduce_fusion.7
  545.5 4.5 copy.347
  550.0 4.5 copy.353
  557.4 4.6 copy.346
  562.0 6.0 fusion.27
  570.6 4.5 copy.352
  575.0 6.0 fusion.24
  586.9 2.9 convert_reduce_fusion.5
  598.2 2.9 multiply_reduce_fusion
  607.2 53.7 %all-reduce.10.cloned.1.call-done = (bf16[4,2,145,768]{3,1,2,0:T(2,128)(2,1)}, bf16[4,2,145,768]{3,1,2,0:T(2,128)(2,1)}) async-done(((bf16[4,2,145,768]{3,1,2,0:T(2,128)(2,1)}, bf16[4,2,145,768]{3,1,2,0:T(2,128)(2,1)}), (bf16[4,2,145,768]{3,1,2,0:T(2,128)(2,1)}, bf16[4,2,145,768]{3,1,2,0:T(2,128)(2,1)})) %all-reduce.10.cloned.1.call-update) | async-done | bytes 3563536
  670.6 3.7 convolution_add_fusion.7
  694.5 4.1 convolution_add_fusion.4
  698.6 8.0 copy.382
  712.0 3.7 add_bitcast_fusion
  716.8 3.2 fusion.142
  720.0 4.5 convolution_add_fusion
  727.3 5.2 convolution_add_fusion.1
  734.4 30.2 %all-reduce.2 = bf16[3072]{0:T(1024)(128)(2,1)S(1)} all-reduce(f32[3072]{0:T(1024)S(1)} %add.456), channel_id=13, replica_groups=mesh['dp'=8,'stream'=4] {'dp'}, use_global_device_ids=true, to_apply=%region_75.78.clone | all-reduce | flops 3072 | bytes 18432
  765.6 22.5 %reduce-scatter.30.cloned.1.call-done = f32[96,10]{1,0:T(8,128)} async-done(((f32[768,10]{1,0:T(8,128)}), f32[96,10]{1,0:T(8,128)}) %reduce-scatter.30.cloned.1.call-update) | async-done | bytes 3856
  789.3 71.6 %reduce-scatter.16.cloned.1.call-done = f32[96,768]{1,0:T(8,128)} async-done(((f32[768,768]{1,0:T(8,128)}), f32[96,768]{1,0:T(8,128)}) %reduce-scatter.16.cloned.1.call-update) | async-done | bytes 294928 | tf_op jit(solution)/shard_map/reduce_scatter | solution.py:375
  862.7 70.1 %reduce-scatter.18.cloned.1.call-done = f32[96,768]{1,0:T(8,128)} async-done(((f32[768,768]{1,0:T(8,128)}), f32[96,768]{1,0:T(8,128)}) %reduce-scatter.18.cloned.1.call-update) | async-done | bytes 294928 | tf_op jit(solution)/shard_map/reduce_scatter | solution.py:376
  934.6 69.9 %reduce-scatter.22.cloned.1.call-done = f32[96,768]{1,0:T(8,128)} async-done(((f32[768,768]{1,0:T(8,128)}), f32[96,768]{1,0:T(8,128)}) %reduce-scatter.22.cloned.1.call-update) | async-done | bytes 294928 | tf_op jit(solution)/shard_map/reduce_scatter | solution.py:378
  1006.3 130.4 %reduce-scatter.28.cloned.1.call-done = f32[96,2304]{1,0:T(8,128)} async-done(((f32[768,2304]{1,0:T(8,128)}), f32[96,2304]{1,0:T(8,128)}) %reduce-scatter.28.cloned.1.call-update) | async-done | bytes 884752
  1139.2 118.5 %reduce-scatter.20.cloned.1.call-done = f32[128,2,768]{0,2,1:T(8,128)} async-done(((f32[1024,2,768]{0,2,1:T(8,128)}), f32[128,2,768]{0,2,1:T(8,128)}) %reduce-scatter.20.cloned.1.call-update) | async-done | bytes 786448 | tf_op jit(solution)/shard_map/reduce_scatter | solution.py:377
  1260.3 164.3 %reduce-scatter.26.cloned.1.call-done = f32[384,768]{1,0:T(8,128)} async-done(((f32[3072,768]{1,0:T(8,128)}), f32[384,768]{1,0:T(8,128)}) %reduce-scatter.26.cloned.1.call-update) | async-done | bytes 1179664 | tf_op jit(solution)/shard_map/reduce_scatter | solution.py:380
  1426.5 164.4 %reduce-scatter.24.cloned.1.call-done = f32[96,3072]{1,0:T(8,128)} async-done(((f32[768,3072]{1,0:T(8,128)}), f32[96,3072]{1,0:T(8,128)}) %reduce-scatter.24.cloned.1.call-update) | async-done | bytes 1179664 | tf_op jit(solution)/shard_map/reduce_scatter | solution.py:379
  1593.1 21.4 %concatenate.32 = bf16[1230432]{0:T(1024)(128)(2,1)S(1)} concatenate(bf16[221184]{0:T(1024)(128)(2,1)S(1)} %reshape.709, bf16[73728]{0:T(1024)(128)(2,1)} %reshape.710, bf16[73728]{0:T(1024)(128)(2,1)} %reshape.711, bf16[196608]{0:T(1024)(128)(2,1)} %reshape.712, bf16[73728]{0:T(1024)(128)(2,1)} %reshape.713, bf16[294912]{0:T(1024)(128)(2,1)} %bitcast.315, ...), dimensions={0} | concatenate | bytes 4921728 | tf_op jit(solution)/shard_map/concatenate | solution.py:304
  1614.5 3.1 convert_element_type.420
  1617.9 56.6 %all-reduce.8.cloned.1.call-done = bf16[4,307608]{1,0:T(4,128)(2,1)} async-done(((bf16[4,307608]{1,0:T(4,128)(2,1)}), bf16[4,307608]{1,0:T(4,128)(2,1)}) %all-reduce.8.cloned.1.call-update) | async-done | bytes 2460880
  1674.5 4.7 dynamic-slice_bitcast_fusion
  1690.0 28.3 %all-gather.33.cloned.1.call-done = bf16[4,1,307608]{2,1,0:T(2,128)(2,1)} async-done(((bf16[1,1,307608]{2,1,0:T(2,128)(2,1)}), bf16[4,1,307608]{2,1,0:T(2,128)(2,1)}) %all-gather.33.cloned.1.call-update) | async-done | bytes 2460880 | tf_op jit(solution)/shard_map/all_gather | solution.py:312
  1718.3 52.1 %convert_reduce_fusion = f32[4,307608]{1,0:T(4,128)} fusion(bf16[4,1,307608]{2,1,0:T(2,128)(2,1)} %all-gather.33.cloned.1.call-done), kind=kLoop, calls=%fused_computation.9 | loop fusion | flops 1230432 | bytes 7382592 | tf_op jit(solution)/shard_map/convert_element_type | solution.py:313
  1770.4 8.2 reshape.718
  1783.9 321.5 %slice.260 = f32[410144,3]{1,0:T(8,128)} reshape(f32[4,307608]{1,0:T(4,128)} %convert_reduce_fusion) | data formatting | bytes 9843456 | tf_op jit(solution)/shard_map/slice | solution.py:320
  (603 shorter events, 220.4 us)
Async XLA Ops:
  7.2 29.1 %copy-start.64 = (bf16[2,1,145,1024]{3,0,2,1:T(2,128)(2,1)S(1)}, bf16[2,1,145,1024]{3,0,2,1:T(2,128)(2,1)}, u32[]{:S(2)}) copy-start(bf16[2,1,145,1024]{3,0,2,1:T(2,128)(2,1)} %param.24) | copy-start | bytes 1781764
  7.2 64.9 %all-gather.19.cloned.1.call-start = ((), (), s32[]{:S(2)}) async-start(), calls=%async_computation.11 | async-start | bytes 3538944 | tf_op jit(solution)/shard_map/all_gather | solution.py:351
  7.9 130.4 %all-gather.15.cloned.1.call-start = ((), (), s32[]{:S(2)}) async-start(), calls=%async_computation.9 | async-start | bytes 3981312 | tf_op jit(solution)/shard_map/all_gather | solution.py:348
  8.7 171.2 %all-gather.17.cloned.1.call-start = ((), (), s32[]{:S(2)}) async-start(), calls=%async_computation.10 | async-start | bytes 1327104 | tf_op jit(solution)/shard_map/all_gather | solution.py:349
  9.4 212.3 %all-gather.23.cloned.1.call-start = ((), (), s32[]{:S(2)}) async-start(), calls=%async_computation.13 | async-start | bytes 1327104 | tf_op jit(solution)/shard_map/all_gather | solution.py:350
  10.0 235.0 %all-gather.21.cloned.1.call-start = ((), (), s32[]{:S(2)}) async-start(), calls=%async_computation.12 | async-start | bytes 2227200 | tf_op jit(solution)/shard_map/all_gather | solution.py:122
  36.3 292.7 %copy-start.101 = (f32[768]{0:T(1024)}, f32[768]{0:T(1024)S(1)}, u32[]{:S(2)}) copy-start(f32[768]{0:T(1024)S(1)} %get-tuple-element.142) | copy-start | bytes 9220
  37.1 37.7 %copy-start.60 = (bf16[1,1,145,1024]{3,0,2,1:T(2,128)(2,1)}, bf16[1,1,145,1024]{3,0,2,1:T(2,128)(2,1)S(1)}, u32[]{:S(2)}) copy-start(bf16[1,1,145,1024]{3,0,2,1:T(2,128)(2,1)S(1)} %get-tuple-element.187) | copy-start | bytes 890884
  37.2 37.7 %copy-start.62 = (bf16[1,1,145,1024]{3,0,2,1:T(2,128)(2,1)}, bf16[1,1,145,1024]{3,0,2,1:T(2,128)(2,1)S(1)}, u32[]{:S(2)}) copy-start(bf16[1,1,145,1024]{3,0,2,1:T(2,128)(2,1)S(1)} %get-tuple-element.188) | copy-start | bytes 890884
  76.9 190.4 %all-gather.31.cloned.1.call-start = ((), (), s32[]{:S(2)}) async-start(), calls=%async_computation.17 | async-start | bytes 2227200 | tf_op jit(solution)/shard_map/all_gather | solution.py:122
  77.0 12.0 copy-start.146
  77.0 27.4 %copy-start.24 = (bf16[2,4,40,768]{3,2,1,0:T(8,128)(2,1)S(1)}, bf16[2,4,40,768]{3,2,1,0:T(8,128)(2,1)}, u32[]{:S(2)}) copy-start(bf16[2,4,40,768]{3,2,1,0:T(8,128)(2,1)} %param.27) | copy-start | bytes 1474564
  78.2 53.0 %copy-start.96 = (bf16[2,4,40,768]{3,2,1,0:T(8,128)(2,1)S(1)}, bf16[2,4,40,768]{3,2,1,0:T(8,128)(2,1)}, u32[]{:S(2)}) copy-start(bf16[2,4,40,768]{3,2,1,0:T(8,128)(2,1)} %param.23) | copy-start | bytes 1474564
  78.2 250.7 %all-gather.25.cloned.1.call-start = ((), (), s32[]{:S(2)}) async-start(), calls=%async_computation.14 | async-start | bytes 1327104 | tf_op jit(solution)/shard_map/all_gather | solution.py:352
  79.0 311.1 %all-gather.27.cloned.1.call-start = ((), (), s32[]{:S(2)}) async-start(), calls=%async_computation.15 | async-start | bytes 5308416 | tf_op jit(solution)/shard_map/all_gather | solution.py:353
  79.7 51.5 %copy-start.154 = (u32[32]{0:T(128)S(1)}, u32[32]{0:T(128)}, u32[]{:S(2)}) copy-start(u32[32]{0:T(128)} %constant.189) | copy-start | bytes 388
  79.7 390.5 %all-gather.29.cloned.1.call-start = ((), (), s32[]{:S(2)}) async-start(), calls=%async_computation.16 | async-start | bytes 5308416 | tf_op jit(solution)/shard_map/all_gather | solution.py:354
  80.5 580.4 %all-reduce.10.cloned.1.call-start = ((), (), s32[]{:S(2)}) async-start(), calls=%async_computation.29 | async-start | bytes 7127040
  87.6 53.6 %copy-start.106 = (f32[160]{0:T(256)}, f32[160]{0:T(256)S(1)}, u32[]{:S(2)}) copy-start(f32[160]{0:T(256)S(1)} %get-tuple-element.168) | copy-start | bytes 1924
  87.6 53.6 %copy-start.108 = (f32[160]{0:T(256)}, f32[160]{0:T(256)S(1)}, u32[]{:S(2)}) copy-start(f32[160]{0:T(256)S(1)} %get-tuple-element.214) | copy-start | bytes 1924
  131.1 19.5 copy-start.137
  131.2 48.7 %copy-start.58 = (bf16[1,4,40,768]{3,2,1,0:T(8,128)(2,1)}, bf16[1,4,40,768]{3,2,1,0:T(8,128)(2,1)S(1)}, u32[]{:S(2)}) copy-start(bf16[1,4,40,768]{3,2,1,0:T(8,128)(2,1)S(1)} %get-tuple-element.196) | copy-start | bytes 737284
  131.2 96.3 %copy-start.52 = (bf16[1,4,40,768]{3,2,1,0:T(8,128)(2,1)}, bf16[1,4,40,768]{3,2,1,0:T(8,128)(2,1)S(1)}, u32[]{:S(2)}) copy-start(bf16[1,4,40,768]{3,2,1,0:T(8,128)(2,1)S(1)} %get-tuple-element.197) | copy-start | bytes 737284
  152.7 29.2 %copy-start.85 = (bf16[12,64,160]{2,1,0:T(8,128)(2,1)}, bf16[12,64,160]{2,1,0:T(8,128)(2,1)S(1)}, u32[]{:S(2)}) copy-start(bf16[12,64,160]{2,1,0:T(8,128)(2,1)S(1)} %convolution_convert_fusion.5) | copy-start | bytes 737284
  183.8 42.0 %copy-start.75 = (f32[12,160,160]{1,2,0:T(8,128)}, f32[12,160,160]{1,2,0:T(8,128)S(1)}, u32[]{:S(2)}) copy-start(f32[12,160,160]{1,2,0:T(8,128)S(1)} %get-tuple-element.239) | copy-start | bytes 3686404
  183.8 42.0 %copy-start.113 = (f32[12,160]{1,0:T(8,128)}, f32[12,160]{1,0:T(8,128)S(1)}, u32[]{:S(2)}) copy-start(f32[12,160]{1,0:T(8,128)S(1)} %get-tuple-element.238) | copy-start | bytes 23044
  228.9 325.5 %copy-start.99 = (f32[160]{0:T(256)}, f32[160]{0:T(256)S(1)}, u32[]{:S(2)}) copy-start(f32[160]{0:T(256)S(1)} %add_rsqrt_fusion.2) | copy-start | bytes 1924
  251.9 22.8 %copy-start.144 = (pred[4]{0:T(512)(128)(4,1)S(1)}, pred[4]{0:T(512)(128)(4,1)}, u32[]{:S(2)}) copy-start(pred[4]{0:T(512)(128)(4,1)} %get-tuple-element.170) | copy-start | bytes 16
  251.9 22.8 %copy-start.145 = (pred[4]{0:T(512)(128)(4,1)S(1)}, pred[4]{0:T(512)(128)(4,1)}, u32[]{:S(2)}) copy-start(pred[4]{0:T(512)(128)(4,1)} %get-tuple-element.218) | copy-start | bytes 16
  306.1 22.9 %copy-start.65 = (bf16[160,768]{1,0:T(8,128)(2,1)}, bf16[160,768]{1,0:T(8,128)(2,1)S(1)}, u32[]{:S(2)}) copy-start(bf16[160,768]{1,0:T(8,128)(2,1)S(1)} %convert_element_type.348) | copy-start | bytes 737284
  332.3 162.4 %copy-start.104 = (f32[160]{0:T(256)}, f32[160]{0:T(256)S(1)}, u32[]{:S(2)}) copy-start(f32[160]{0:T(256)S(1)} %broadcast_multiply_fusion.13) | copy-start | bytes 1924
  333.2 156.1 %copy-start.102 = (f32[160]{0:T(256)}, f32[160]{0:T(256)S(1)}, u32[]{:S(2)}) copy-start(f32[160]{0:T(256)S(1)} %add_rsqrt_fusion.4) | copy-start | bytes 1924
  333.2 156.1 %copy-start.110 = (f32[160]{0:T(256)}, f32[160]{0:T(256)S(1)}, u32[]{:S(2)}) copy-start(f32[160]{0:T(256)S(1)} %add_rsqrt_fusion.1) | copy-start | bytes 1924
  390.0 80.2 %copy-start.142 = (f32[768]{0:T(1024)S(1)}, f32[768]{0:T(1024)}, u32[]{:S(2)}) copy-start(f32[768]{0:T(1024)} %get-tuple-element.140) | copy-start | bytes 9220
  390.0 84.7 %slice-start = ((s8[4718592]{0:T(1024)(128)(4,1)}), s8[524288]{0:T(1024)(128)(4,1)S(1)}, s32[]{:S(2)}) async-start(s8[4718592]{0:T(1024)(128)(4,1)} %bitcast.294), calls=%async_computation.30 | async-start | bytes 1048576
  477.1 9.6 copy-start.34
  586.1 178.5 %reduce-scatter.32.cloned.1.call-start = ((), (), s32[]{:S(2)}) async-start(), calls=%async_computation.27 | async-start | bytes 442368
  586.9 9.6 copy-start.84
  604.2 61.3 %copy-start.124 = (f32[768,1]{0,1:T(1,128)S(1)}, f32[768,1]{0,1:T(1,128)}, u32[]{:S(2)}) copy-start(f32[768,1]{0,1:T(1,128)} %stack.187) | copy-start | bytes 9220
  604.2 61.3 %copy-start.125 = (f32[768,1]{0,1:T(1,128)S(1)}, f32[768,1]{0,1:T(1,128)}, u32[]{:S(2)}) copy-start(f32[768,1]{0,1:T(1,128)} %stack.186) | copy-start | bytes 9220
  604.2 61.3 %copy-start.126 = (f32[768,1]{0,1:T(1,128)S(1)}, f32[768,1]{0,1:T(1,128)}, u32[]{:S(2)}) copy-start(f32[768,1]{0,1:T(1,128)} %stack.184) | copy-start | bytes 9220
  604.2 61.3 %copy-start.127 = (f32[768,1]{0,1:T(1,128)S(1)}, f32[768,1]{0,1:T(1,128)}, u32[]{:S(2)}) copy-start(f32[768,1]{0,1:T(1,128)} %stack.185) | copy-start | bytes 9220
  604.2 61.3 %copy-start.128 = (f32[768,1]{0,1:T(1,128)S(1)}, f32[768,1]{0,1:T(1,128)}, u32[]{:S(2)}) copy-start(f32[768,1]{0,1:T(1,128)} %stack.181) | copy-start | bytes 9220
  604.2 61.3 %copy-start.129 = (f32[768,1]{0,1:T(1,128)S(1)}, f32[768,1]{0,1:T(1,128)}, u32[]{:S(2)}) copy-start(f32[768,1]{0,1:T(1,128)} %stack.180) | copy-start | bytes 9220
  604.2 61.3 %copy-start.131 = (f32[768,1]{0,1:T(1,128)S(1)}, f32[768,1]{0,1:T(1,128)}, u32[]{:S(2)}) copy-start(f32[768,1]{0,1:T(1,128)} %stack.182) | copy-start | bytes 9220
  604.2 61.3 %copy-start.133 = (f32[768,1]{0,1:T(1,128)S(1)}, f32[768,1]{0,1:T(1,128)}, u32[]{:S(2)}) copy-start(f32[768,1]{0,1:T(1,128)} %stack.179) | copy-start | bytes 9220
  604.2 61.3 %copy-start.134 = (f32[768,1]{0,1:T(1,128)S(1)}, f32[768,1]{0,1:T(1,128)}, u32[]{:S(2)}) copy-start(f32[768,1]{0,1:T(1,128)} %stack.177) | copy-start | bytes 9220
  604.2 62.6 %copy-start.123 = (f32[768,1]{0,1:T(1,128)S(1)}, f32[768,1]{0,1:T(1,128)}, u32[]{:S(2)}) copy-start(f32[768,1]{0,1:T(1,128)} %stack.200) | copy-start | bytes 9220
  604.3 62.6 %copy-start.130 = (f32[768,1]{0,1:T(1,128)S(1)}, f32[768,1]{0,1:T(1,128)}, u32[]{:S(2)}) copy-start(f32[768,1]{0,1:T(1,128)} %stack.195) | copy-start | bytes 9220
  604.3 62.5 %copy-start.132 = (f32[768,1]{0,1:T(1,128)S(1)}, f32[768,1]{0,1:T(1,128)}, u32[]{:S(2)}) copy-start(f32[768,1]{0,1:T(1,128)} %stack.192) | copy-start | bytes 9220
  607.1 63.5 %copy-start.46 = (f32[160,768]{1,0:T(8,128)S(1)}, f32[160,768]{1,0:T(8,128)}, u32[]{:S(2)}) copy-start(f32[160,768]{1,0:T(8,128)} %copy-done.45) | copy-start | bytes 1474564
  607.1 181.0 %reduce-scatter.30.cloned.1.call-start = ((), (), s32[]{:S(2)}) async-start(), calls=%async_computation.26 | async-start | bytes 442368
  670.6 190.4 %reduce-scatter.16.cloned.1.call-start = ((), (), s32[]{:S(2)}) async-start(), calls=%async_computation.18 | async-start | bytes 2654208 | tf_op jit(solution)/shard_map/reduce_scatter | solution.py:375
  674.3 258.5 %reduce-scatter.18.cloned.1.call-start = ((), (), s32[]{:S(2)}) async-start(), calls=%async_computation.19 | async-start | bytes 2654208 | tf_op jit(solution)/shard_map/reduce_scatter | solution.py:376
  677.9 326.6 %reduce-scatter.22.cloned.1.call-start = ((), (), s32[]{:S(2)}) async-start(), calls=%async_computation.21 | async-start | bytes 2654208 | tf_op jit(solution)/shard_map/reduce_scatter | solution.py:378
  681.4 455.2 %reduce-scatter.28.cloned.1.call-start = ((), (), s32[]{:S(2)}) async-start(), calls=%async_computation.25 | async-start | bytes 7962624
  706.6 551.1 %reduce-scatter.20.cloned.1.call-start = ((), (), s32[]{:S(2)}) async-start(), calls=%async_computation.20 | async-start | bytes 7077888 | tf_op jit(solution)/shard_map/reduce_scatter | solution.py:377
  715.8 708.8 %reduce-scatter.26.cloned.1.call-start = ((), (), s32[]{:S(2)}) async-start(), calls=%async_computation.23 | async-start | bytes 10616832 | tf_op jit(solution)/shard_map/reduce_scatter | solution.py:380
  724.6 866.3 %reduce-scatter.24.cloned.1.call-start = ((), (), s32[]{:S(2)}) async-start(), calls=%async_computation.22 | async-start | bytes 10616832 | tf_op jit(solution)/shard_map/reduce_scatter | solution.py:379
  732.5 942.0 %all-reduce.8.cloned.1.call-start = ((), (), s32[]{:S(2)}) async-start(), calls=%async_computation.28 | async-start | bytes 4923392
  1617.6 63.5 %copy-start.13 = (bf16[3,768,768]{2,1,0:T(8,128)(2,1)S(1)}, bf16[3,768,768]{2,1,0:T(8,128)(2,1)}, u32[]{:S(2)}) copy-start(bf16[3,768,768]{2,1,0:T(8,128)(2,1)} %all-gather.15.cloned.1.call-done) | copy-start | bytes 10616836
  1617.6 100.7 %all-gather.33.cloned.1.call-start = ((), (), s32[]{:S(2)}) async-start(), calls=%async_computation.24 | async-start | bytes 6154240 | tf_op jit(solution)/shard_map/all_gather | solution.py:312
  1783.9 321.5 %slice-start.2 = ((f32[1230432]{0:T(1024)}), f32[960]{0:T(1024)S(1)}, s32[]{:S(2)}) async-start(f32[1230432]{0:T(1024)} %reshape.718), calls=%async_computation.32 | async-start | bytes 8192 | tf_op jit(solution)/shard_map/slice | solution.py:320
  1783.9 322.3 %slice-start.3 = ((f32[1230432]{0:T(1024)}), f32[196608]{0:T(1024)S(1)}, s32[]{:S(2)}) async-start(f32[1230432]{0:T(1024)} %reshape.718), calls=%async_computation.33 | async-start | bytes 1572864 | tf_op jit(solution)/shard_map/slice | solution.py:320
  (117 other events, 295.4 us)
Sparse Core Ops, SparseCore 0:
  10.2 61.8 all-gather.18
  74.3 63.9 all-gather.14
  140.5 39.3 all-gather.16
  181.9 39.8 all-gather.22
  223.7 21.2 all-gather.20
  246.4 20.8 all-gather.30
  269.5 39.3 all-gather.24
  311.1 78.9 all-gather.26
  392.2 78.0 all-gather.28
  586.3 74.5 all-reduce.9
  664.5 59.6 reduce-scatter.31
  727.6 60.4 reduce-scatter.29
  792.0 68.8 reduce-scatter.15
  864.7 68.0 reduce-scatter.17
  936.5 67.8 reduce-scatter.21
  1008.5 128.1 reduce-scatter.27
  1140.1 117.5 reduce-scatter.19
  1261.2 163.4 reduce-scatter.25
  1428.2 162.5 reduce-scatter.23
  1617.7 56.7 all-reduce.7
  1679.3 38.9 all-gather.32
where the time goes:
time: 2140 us; the launch traced here: 2130 us
  waiting for transfers between devices  1220 us (57%)
  local copies, waits for them, and re-layouts  530 us (25%)
  matrix products  163 us (8%)
  other arithmetic  98.1 us (5%)
  blocking collectives  93.7 us (4%)
    slice x10, local copies, waits for them, and re-layouts, stream_total(): results.append(combined[offset:offset + count].reshape(piece.shape))  326 us
    unnamed x26, waiting for transfers between devices  268 us
    reduce_scatter x1, waiting for transfers between devices, on_device(): lax.psum_scatter(totals[5], 'dp', scatter_dimension=0, tiled=True)  164 us
    reduce_scatter x1, waiting for transfers between devices, on_device(): lax.psum_scatter(totals[6], 'dp', scatter_dimension=0, tiled=True)  164 us
    reduce_scatter x1, waiting for transfers between devices, on_device(): lax.psum_scatter(totals[3], 'dp', scatter_dimension=0, tiled=True)  119 us
    all_gather x1, waiting for transfers between devices, on_device(): lax.all_gather(ffn_out, 'dp', axis=0, tiled=True)  75.5 us
    reduce_scatter x1, waiting for transfers between devices, on_device(): lax.psum_scatter(totals[1], 'dp', scatter_dimension=0, tiled=True)  71.6 us
    reduce_scatter x1, waiting for transfers between devices, on_device(): lax.psum_scatter(totals[2], 'dp', scatter_dimension=0, tiled=True)  70.1 us
  transfers between devices with their start and end apart: 21, of which 19 were waited for; matrix products, arithmetic and copies ran while one was open for 11% of the time, Pallas kernels for 0%

commit v1 on v0

--- a/solution.py
+++ b/solution.py
@@ -1,11 +1,209 @@
+import functools
 import math
 
 import jax
 import jax.numpy as jnp
 from jax import lax
+from jax.experimental import pallas as pl
+from jax.experimental.pallas import tpu as pltpu
 from jax.sharding import PartitionSpec as P
 
 HEADS = 12
+LANES = 384
+
+CORE = ((0, 1), (1, 0), (2, 3), (3, 2))
+ACROSS = ((0, 2), (2, 0), (1, 3), (3, 1))
+BESIDE = ((0, 1), (1, 0), (2, 3), (3, 2), (4, 5), (5, 4), (6, 7), (7, 6))
+PAIR = ((0, 2), (2, 0), (1, 3), (3, 1), (4, 6), (6, 4), (5, 7), (7, 5))
+MIDDLE = ((2, 4), (4, 2), (3, 5), (5, 3))
+OUTWARD = ((2, 0), (3, 1), (4, 6), (5, 7))
+INWARD = ((0, 2), (1, 3), (6, 4), (7, 5))
+
+
+def pick(array, index, axis=0):
+    return lax.dynamic_index_in_dim(array, index, axis, keepdims=False)
+
+
+def place():
+    dp_at, stream_at = lax.axis_index("dp"), lax.axis_index("stream")
+    return dp_at // 2, dp_at % 2, stream_at // 2, stream_at % 2
+
+
+def pack_shard(shard, units):
+    if shard.ndim == 2:
+        rows, columns = shard.shape
+        split = shard.reshape(2, rows // 2, 2, units, LANES).transpose(2, 0, 3, 1, 4)
+    else:
+        _, rows, columns = shard.shape
+        split = shard.reshape(units, 2, rows // 2, 2, LANES).transpose(3, 1, 0, 2, 4)
+    return split.reshape(2, 2, units * rows // 2, LANES)
+
+
+def gather_pieces(own_both):
+    _, _, x_at, core_at = place()
+    z_at = lax.axis_index("dp") // 2
+    own = pick(own_both, core_at)
+    mate = lax.ppermute(own, "dp", PAIR)
+    pair = jnp.stack((own, mate))
+    middle = lax.ppermute(pair, "dp", MIDDLE)
+    outer = lax.ppermute(middle, "dp", OUTWARD)
+    inside = (z_at == 1) | (z_at == 2)
+    other = jnp.where(inside, middle, outer)
+    near = lax.ppermute(pick(pair, x_at, 1), "dp", BESIDE)
+    far = lax.ppermute(pick(other, x_at, 1), "dp", BESIDE)
+    near_x = lax.ppermute(near, "stream", ACROSS)
+    far_x = lax.ppermute(far, "stream", ACROSS)
+    mine = (mate, other, near, far, near_x, far_x)
+    theirs = tuple(lax.ppermute(piece, "stream", CORE) for piece in mine)
+    return (own_both, *mine, *theirs)
+
+
+def assemble_kernel(units, *refs):
+    n_out = len(units)
+    own_both, mate, other, near, far, near_x, far_x, *theirs = refs[:13]
+    outs = refs[13 : 13 + n_out]
+    sems = refs[13 + n_out]
+    dp_at, stream_at = lax.axis_index("dp"), lax.axis_index("stream")
+    z_at, y_at = dp_at // 2, dp_at % 2
+    x_at, core_at = stream_at // 2, stream_at % 2
+    copies = []
+
+    def whole(piece, z_from, y_from, x_from, core_from):
+        row = 0
+        for (count, depth), out in zip(units, outs):
+            start = (z_from * 2 + y_from) * (2 * depth) + x_from * depth
+            for unit in range(count):
+                copies.append(
+                    pltpu.make_async_copy(
+                        piece.at[pl.ds(row, depth)],
+                        out.at[core_from, unit, pl.ds(pl.multiple_of(start, 16), depth)],
+                        sems.at[len(copies)],
+                    )
+                )
+                copies[-1].start()
+                row += depth
+
+    for core_from in range(2):
+        for x_from in range(2):
+            whole(own_both.at[core_from, x_from], z_at, y_at, x_from, core_from)
+    base = 2 - (z_at // 2) * 2
+    others = (jnp.where(z_at < 2, 2, 1), jnp.where(z_at < 2, 3, 0))
+    pair_z = (z_at, z_at + 1 - 2 * (z_at % 2))
+    for group, core_from in (((mate, other, near, far, near_x, far_x), core_at), (theirs, 1 - core_at)):
+        g_mate, g_other, g_near, g_far, g_near_x, g_far_x = group
+        for x_from in range(2):
+            whole(g_mate.at[x_from], pair_z[1], y_at, x_from, core_from)
+            for j in range(2):
+                whole(g_other.at[j, x_from], others[j], y_at, x_from, core_from)
+        for j in range(2):
+            whole(g_near.at[j], pair_z[j], 1 - y_at, x_at, core_from)
+            whole(g_far.at[j], others[j], 1 - y_at, x_at, core_from)
+            whole(g_near_x.at[j], pair_z[j], 1 - y_at, 1 - x_at, core_from)
+            whole(g_far_x.at[j], others[j], 1 - y_at, 1 - x_at, core_from)
+    for copy in copies:
+        copy.wait()
+
+
+def gather_group(shards, units):
+    packed = [
+        shard if shard.ndim == 4 else pack_shard(shard, count)
+        for shard, (count, _) in zip(shards, units)
+    ]
+    own_both = jnp.concatenate(packed, axis=2)
+    dp = lax.axis_size("dp")
+    if dp != 8 or lax.axis_size("stream") != 4:
+        whole = lax.all_gather(own_both, "dp", axis=0, tiled=False)
+        results = []
+        row = 0
+        for count, depth in units:
+            part = whole[:, :, :, row : row + count * depth]
+            part = part.reshape(dp, 2, 2, count, depth, LANES).transpose(1, 3, 0, 2, 4, 5)
+            results.append(part.reshape(2, count, dp * 2 * depth, LANES))
+            row += count * depth
+        return results
+    pieces = gather_pieces(own_both)
+    total = sum(count for count, _ in units)
+    return pl.pallas_call(
+        functools.partial(assemble_kernel, units),
+        out_shape=[
+            jax.ShapeDtypeStruct((2, count, dp * 2 * depth, LANES), own_both.dtype)
+            for count, depth in units
+        ],
+        in_specs=[pl.BlockSpec(memory_space=pl.ANY)] * 13,
+        out_specs=[pl.BlockSpec(memory_space=pltpu.VMEM)] * len(units),
+        scratch_shapes=[pltpu.SemaphoreType.DMA((32 * total,))],
+        compiler_params=pltpu.CompilerParams(vmem_limit_bytes=40 * 2**20),
+        name="assemble",
+    )(*pieces)
+
+
+def low(value):
+    return value.astype(jnp.bfloat16)
+
+
+def wide(value):
+    return value.astype(jnp.float32)
+
+
+def reduce_group(mine, sibling):
+    z_at, y_at, x_at, core_at = place()
+    came = lax.ppermute(sibling, "stream", CORE)
+    mine_y, came_y = pick(mine, 1 - y_at, 1), pick(came, 1 - y_at, 1)
+    hop = low(wide(pick(mine_y, 1 - x_at, 1)) + wide(pick(came_y, 1 - x_at, 1)))
+    from_x = lax.ppermute(hop, "stream", ACROSS)
+    hop = low(wide(pick(mine_y, x_at, 1)) + wide(pick(came_y, x_at, 1)) + wide(from_x))
+    from_y = lax.ppermute(hop, "dp", BESIDE)
+    here = jnp.arange(2)[None, :, None, None] == x_at
+    held = low(
+        wide(pick(mine, y_at, 1))
+        + wide(pick(came, y_at, 1))
+        + jnp.where(here, wide(from_y)[:, None], 0.0)
+    )
+    side = z_at // 2
+    halves = held.reshape(2, 2, *held.shape[1:])
+    hop = pick(halves, 1 - side)
+    first = lax.ppermute(hop, "dp", INWARD)
+    second = lax.ppermute(low(wide(hop) + wide(first)), "dp", MIDDLE)
+    kept = pick(halves, side)
+    spot = z_at % 2
+    hop = low(wide(pick(kept, 1 - spot)) + wide(pick(second, 1 - spot)))
+    third = lax.ppermute(hop, "dp", PAIR)
+    total = low(wide(pick(kept, spot)) + wide(pick(second, spot)) + wide(third))
+    from_x = lax.ppermute(total, "stream", ACROSS)
+    total = low(wide(total) + wide(from_x))
+    total = lax.optimization_barrier(total)
+    other = lax.ppermute(total, "stream", CORE)
+    first_half = jnp.where(core_at == 0, total, other)
+    second_half = jnp.where(core_at == 0, other, total)
+    return jnp.stack((first_half, second_half))
+
+
+def reduce_any(both):
+    dp = lax.axis_size("dp")
+    if dp != 8 or lax.axis_size("stream") != 4:
+        own = lax.psum_scatter(both, "dp", scatter_dimension=1, tiled=True)[:, 0]
+        return lax.psum(own, "stream")
+    core_at = lax.axis_index("stream") % 2
+    both = both.reshape(2, 4, 2, *both.shape[2:])
+    return reduce_group(pick(both, core_at), pick(both, 1 - core_at))
+
+
+def pack_grad(grad, units):
+    dp = lax.axis_size("dp")
+    if grad.ndim == 2:
+        depth = grad.shape[0] // (2 * dp)
+        split = grad.reshape(dp, 2, depth, 2, units, LANES).transpose(3, 0, 1, 4, 2, 5)
+    else:
+        depth = grad.shape[1] // (2 * dp)
+        split = grad.reshape(units, dp, 2, depth, 2, LANES).transpose(4, 1, 2, 0, 3, 5)
+    return low(split).reshape(2, dp, 2, units * depth, LANES)
+
+
+def unpack_shard(packed, units, depth, flat):
+    split = packed.reshape(2, 2, units, depth, LANES)
+    if flat:
+        return wide(split.transpose(1, 3, 0, 2, 4).reshape(2 * depth, 2 * units * LANES))
+    return wide(split.transpose(2, 1, 3, 0, 4).reshape(units, 2 * depth, 2 * LANES))
 
 
 EPSILON = 1e-06
@@ -67,7 +265,7 @@
     )
 
 
-def micro_batch(weights, word_rows, pixels, lengths, images, upstream_rows):
+def micro_batch(weights, word_rows, pixels, lengths, images, micro_of_row, upstream_rows):
     (
         self_qkv,
         self_out,
@@ -119,9 +317,11 @@
     cross_query_heads = cross_query.reshape(row_count, seq_len, HEADS, head_size)
     image_kv = jnp.einsum("ipv,jvd->jipd", pixels, cross_kv, preferred_element_type=jnp.float32)
     own_kv = jnp.stack((image_kv[0], image_kv[1] + bias_rows[5])).astype(jnp.bfloat16)
-    group_kv = lax.all_gather(own_kv, "stream", axis=1, tiled=True)
-    group_count = group_kv.shape[1]
-    row_kv = jnp.take(group_kv, images, axis=1)
+    beside_kv = lax.ppermute(own_kv, "stream", CORE)
+    across_kv = lax.ppermute(jnp.stack((own_kv, beside_kv)), "stream", ACROSS)
+    group_kv = jnp.concatenate((own_kv[None], beside_kv[None], across_kv))
+    group_count = group_kv.shape[0]
+    row_kv = jnp.stack(tuple(group_kv[images, j, micro_of_row] for j in range(2)))
     row_keys = row_kv[0].reshape(row_count, patch_count, HEADS, head_size)
     row_values = row_kv[1].reshape(row_count, patch_count, HEADS, head_size)
     cross_scores = (
@@ -210,19 +410,20 @@
             grad_row_values.reshape(row_count, patch_count, width_all),
         )
     )
-    selector = (images[:, None] == jnp.arange(group_count, dtype=jnp.int32)[None, :]).astype(
-        jnp.float32
-    )
-    grad_group_kv = jnp.einsum("ri,jrpd->ijpd", selector, grad_rows_kv, precision=HIGHEST)
-    grad_own_kv = lax.psum_scatter(
-        grad_group_kv.astype(jnp.bfloat16), "stream", scatter_dimension=0, tiled=True
-    )
+    selector = (
+        (images[:, None, None] == jnp.arange(group_count, dtype=jnp.int32)[None, :, None])
+        & (micro_of_row[:, None, None] == jnp.arange(pixels.shape[0])[None, None, :])
+    ).astype(jnp.float32)
+    grad_group_kv = jnp.einsum("rim,jrpd->ijmpd", selector, grad_rows_kv, precision=HIGHEST)
+    from_x = lax.ppermute(low(grad_group_kv[2:]), "stream", ACROSS)
+    grad_pair = grad_group_kv[:2] + wide(from_x)
+    grad_own_kv = low(grad_pair[0] + wide(lax.ppermute(low(grad_pair[1]), "stream", CORE)))
     grad_cross_kv = jnp.einsum(
-        "ipv,ijpd->vjd", pixels, grad_own_kv, preferred_element_type=jnp.float32
-    )
-    value_bias = jnp.sum(grad_own_kv[:, 1].astype(jnp.float32), axis=(0, 1))
+        "ipv,jipd->jvd", pixels, grad_own_kv, preferred_element_type=jnp.float32
+    )
+    value_bias = jnp.sum(grad_own_kv[1].astype(jnp.float32), axis=(0, 1))
     grad_pixels = jnp.einsum(
-        "ijpd,jvd->ipv", grad_own_kv, cross_kv, preferred_element_type=jnp.float32
+        "jipd,jvd->ipv", grad_own_kv, cross_kv, preferred_element_type=jnp.float32
     ).astype(jnp.bfloat16)
     grad_cross_q = contract_rows(first_low, grad_cross_query)
     grad_first_total = grad_second + contract_last(grad_cross_query, cross_q)
@@ -257,7 +458,7 @@
         .reshape(3, tokens, width_all)
     )
     grad_self_qkv = jnp.einsum(
-        "nd,jne->dje", flat_tokens, grad_qkv_low, preferred_element_type=jnp.float32
+        "nd,jne->jde", flat_tokens, grad_qkv_low, preferred_element_type=jnp.float32
     )
     grad_text = grad_first + jnp.einsum(
         "jne,jde->nd", grad_qkv_low, self_qkv, preferred_element_type=jnp.float32
@@ -274,10 +475,9 @@
             second_shift,
             column_sum(grad_lowered),
             third_shift,
-        ),
-        axis=1,
-    )
-    grad_gains = jnp.stack((first_gain, second_gain, third_gain), axis=1)
+        )
+    )
+    grad_gains = jnp.stack((first_gain, second_gain, third_gain))
     grads = (
         grad_self_qkv,
         grad_self_out,
@@ -296,30 +496,6 @@
         grad_pixels,
         grads,
     )
-
-
-def stream_total(shards):
-    streams = lax.axis_size("stream")
-    flat_parts = [piece.reshape(-1) for piece in shards]
-    joined = jnp.concatenate(flat_parts)
-    length = joined.shape[0]
-    padded_len = -(-length // streams) * streams
-    joined = jnp.pad(joined, (0, padded_len - length)).reshape(streams, padded_len // streams)
-    own_share = lax.psum_scatter(
-        joined.astype(jnp.bfloat16), "stream", scatter_dimension=0, tiled=True
-    ).astype(jnp.float32)
-    combined = (
-        lax.all_gather(own_share.astype(jnp.bfloat16), "stream", axis=0, tiled=True)
-        .astype(own_share.dtype)
-        .reshape(-1)
-    )
-    results = []
-    offset = 0
-    for piece in shards:
-        count = piece.size
-        results.append(combined[offset : offset + count].reshape(piece.shape))
-        offset = offset + count
-    return results
 
 
 def on_device(
@@ -339,68 +515,86 @@
     norm_gains,
     ffn_bias,
 ):
-    output_list = []
-    text_list = []
-    patch_list = []
-    totals = None
-    for micro_step in range(text_input.shape[0]):
-        gathered = (
-            lax.all_gather(self_qkv, "dp", axis=1, tiled=True),
-            lax.all_gather(self_out, "dp", axis=0, tiled=True),
-            lax.all_gather(cross_q, "dp", axis=0, tiled=True),
-            lax.all_gather(cross_kv, "dp", axis=1, tiled=True),
-            lax.all_gather(cross_out, "dp", axis=0, tiled=True),
-            lax.all_gather(ffn_in, "dp", axis=0, tiled=True),
-            lax.all_gather(ffn_out, "dp", axis=0, tiled=True),
-            lax.all_gather(biases, "dp", axis=1, tiled=True),
-            lax.all_gather(norm_gains, "dp", axis=1, tiled=True),
-            lax.all_gather(ffn_bias, "dp", axis=0, tiled=True),
-        )
-        output_rows, text_rows, patch_rows, grads = micro_batch(
-            gathered,
-            text_input[micro_step],
-            patch_input[micro_step],
-            text_lengths[micro_step],
-            image_of_row[micro_step],
-            cotangent[micro_step],
-        )
-        output_list.append(output_rows)
-        text_list.append(text_rows)
-        patch_list.append(patch_rows)
-        totals = (
-            grads if totals is None else tuple((left + right for left, right in zip(totals, grads)))
-        )
-    totals = (
-        lax.psum_scatter(totals[0], "dp", scatter_dimension=0, tiled=True),
-        lax.psum_scatter(totals[1], "dp", scatter_dimension=0, tiled=True),
-        lax.psum_scatter(totals[2], "dp", scatter_dimension=0, tiled=True),
-        lax.psum_scatter(totals[3], "dp", scatter_dimension=0, tiled=True),
-        lax.psum_scatter(totals[4], "dp", scatter_dimension=0, tiled=True),
-        lax.psum_scatter(totals[5], "dp", scatter_dimension=0, tiled=True),
-        lax.psum_scatter(totals[6], "dp", scatter_dimension=0, tiled=True),
-        lax.psum_scatter(totals[7], "dp", scatter_dimension=0, tiled=True),
-        lax.psum_scatter(totals[8], "dp", scatter_dimension=0, tiled=True),
-        lax.psum_scatter(totals[9], "dp", scatter_dimension=0, tiled=True),
-    )
-    summed = stream_total(list(totals))
-    grad_self_qkv = jnp.transpose(summed[0], (1, 0, 2))
-    grad_cross_kv = jnp.transpose(summed[3], (1, 0, 2))
-    grad_biases = jnp.transpose(summed[7])
-    grad_gains = jnp.transpose(summed[8])
+    dp = lax.axis_size("dp")
+    micros, row_count, seq_len, width = text_input.shape
+    part = biases.shape[1]
+    small = jnp.concatenate((biases, norm_gains, ffn_bias.reshape(-1, part)))
+    small_rows = small.shape[0]
+    wide_rows = biases.shape[0] + norm_gains.shape[0]
+    small = jnp.pad(small, ((0, 32 - small_rows), (0, LANES - part)))
+    small = jnp.broadcast_to(small.reshape(2, 16, LANES), (2, 2, 16, LANES))
+    half = width // dp // 2
+    half_v = cross_kv.shape[1] // 2
+    half_f = ffn_out.shape[0] // 2
+    in_units = ffn_in.shape[1] // (2 * LANES)
+    w_qkv, w_small = gather_group((self_qkv, small), ((3, half), (1, 16)))
+    small = w_small[0, 0].reshape(dp, 32, LANES)[:, :small_rows, :part]
+    rows_all = small[:, :wide_rows].transpose(1, 0, 2).reshape(wide_rows, width)
+    bias_all, gain_all = rows_all[: biases.shape[0]], rows_all[biases.shape[0] :]
+    ffn_bias_all = small[:, wide_rows:].reshape(-1)
+
+    w_kv, w_so, w_cq = gather_group((cross_kv, self_out, cross_q), ((2, half_v), (1, half), (1, half)))
+    w_co, w_in = gather_group((cross_out, ffn_in), ((1, half), (in_units, half)))
+    (w_out,) = gather_group((ffn_out,), ((1, half_f),))
+
+    def columns(whole):
+        return whole.transpose(2, 0, 1, 3).reshape(whole.shape[2], -1)
+
+    def stacked(whole):
+        return whole.transpose(1, 2, 0, 3).reshape(whole.shape[1], whole.shape[2], -1)
+
+    weights = (
+        stacked(w_qkv), columns(w_so), columns(w_cq), stacked(w_kv), columns(w_co), columns(w_in),
+        columns(w_out), bias_all, gain_all, ffn_bias_all,
+    )
+    micro_of_row = jnp.repeat(jnp.arange(micros, dtype=jnp.int32), row_count)
+    slots = image_of_row.reshape(-1) ^ lax.axis_index("stream")
+    out_rows, text_rows, patch_rows, grads = micro_batch(
+        weights,
+        text_input.reshape(micros * row_count, seq_len, width),
+        patch_input.reshape(-1, *patch_input.shape[2:]),
+        text_lengths.reshape(-1),
+        slots,
+        micro_of_row,
+        cotangent.reshape(micros * row_count, seq_len, width),
+    )
+    g_qkv, g_so, g_cq, g_kv, g_co, g_in, g_out, g_biases, g_gains, g_ffn_bias = grads
+    r_out = reduce_any(pack_grad(g_out, 1))
+    r_in = reduce_any(pack_grad(g_in, in_units))
+    mid = jnp.concatenate((pack_grad(g_co, 1), pack_grad(g_kv, 2), pack_grad(g_cq, 1), pack_grad(g_so, 1)), axis=3)
+    r_mid = reduce_any(mid)
+    g_small = jnp.concatenate(
+        (
+            jnp.concatenate((g_biases, g_gains)).reshape(wide_rows, dp, part).transpose(1, 0, 2),
+            g_ffn_bias.reshape(dp, -1, part),
+        ),
+        axis=1,
+    )
+    g_small = jnp.pad(low(g_small), ((0, 0), (0, 32 - small_rows), (0, LANES - part)))
+    g_small = g_small.reshape(1, dp, 2, 16, LANES)
+    g_small = jnp.concatenate((g_small, jnp.zeros_like(g_small)))
+    r_qkv = reduce_any(jnp.concatenate((pack_grad(g_qkv, 3), g_small), axis=3))
+    at = 0
+    mids = []
+    for units, depth, flat in ((1, half, True), (2, half_v, False), (1, half, True), (1, half, True)):
+        mids.append(unpack_shard(r_mid[:, :, at : at + units * depth], units, depth, flat))
+        at += units * depth
+    s_co, s_kv, s_cq, s_so = mids
+    g_small = wide(r_qkv[0, :, 3 * half :, :part].reshape(32, part)[:small_rows])
     return (
-        jnp.stack(output_list),
-        jnp.stack(text_list),
-        jnp.stack(patch_list),
-        grad_self_qkv,
-        summed[1],
-        summed[2],
-        grad_cross_kv,
-        summed[4],
-        summed[5],
-        summed[6],
-        grad_biases,
-        grad_gains,
-        summed[9],
+        out_rows.reshape(text_input.shape),
+        text_rows.reshape(text_input.shape),
+        patch_rows.reshape(patch_input.shape),
+        unpack_shard(r_qkv[:, :, : 3 * half], 3, half, False),
+        s_so,
+        s_cq,
+        s_kv,
+        s_co,
+        unpack_shard(r_in, in_units, half, True),
+        unpack_shard(r_out, 1, half_f, True),
+        g_small[: biases.shape[0]],
+        g_small[biases.shape[0] : wide_rows],
+        g_small[wide_rows:].reshape(-1),
     )
 
 

time: 2140 us -> 764 us (0.36)
  waiting for transfers between devices: 1220 us -> 162 us
  local copies, waits for them, and re-layouts: 530 us -> 272 us
  starting transfers between devices: 1.64 us -> 117 us
  blocking collectives: 93.7 us -> 0 us
  matrix products: 163 us -> 103 us
  other arithmetic: 98.1 us -> 73.3 us
  Pallas kernels: 0 us -> 24.3 us
    reduce_scatter x6 -> x0, waiting for transfers between devices: 659 us -> none  [the longest x1 164 us: on_device(): lax.psum_scatter(totals[5], 'dp', scatter_dimension=0, tiled=True)]
    slice x19 -> x10, local copies, waits for them, and re-layouts: 354 us -> 6.23 us  [the longest x1 3.05 us: micro_batch(): from_x = lax.ppermute(low(grad_group_kv[2:]), 'stream', ACROSS)]
    all_gather x10 -> x0, waiting for transfers between devices: 296 us -> none  [the longest x1 75.5 us: on_device(): lax.all_gather(ffn_out, 'dp', axis=0, tiled=True)]
    unnamed x26 -> x0, waiting for transfers between devices: 268 us -> none
    ppermute x0 -> x88, waiting for transfers between devices: none -> 162 us  [the longest x4 52.8 us: gather_pieces(): outer = lax.ppermute(middle, 'dp', OUTWARD)]
    ppermute x0 -> x88, starting transfers between devices: none -> 117 us  [the longest x4 28.6 us: reduce_group(): other = lax.ppermute(total, 'stream', CORE)]
    all_gather x3 -> x0, blocking collectives: 63.5 us -> none  [the longest x1 25.6 us: on_device(): lax.all_gather(biases, 'dp', axis=1, tiled=True)]
    convert_element_type x5 -> x21, local copies, waits for them, and re-layouts: 8.4 us -> 59.3 us  [the longest x10 51.6 us: low(): return value.astype(jnp.bfloat16)]
  transfers between devices with their start and end apart: 21 -> 88, of which waited for: 19 -> 19; matrix products, arithmetic and copies ran while one was open for 11% -> 33% of each run, Pallas kernels for 0% -> 3%
where the time goes in v1:
time: 764 us; the launch traced here: 755 us
  local copies, waits for them, and re-layouts  272 us (36%)
  waiting for transfers between devices  162 us (21%)
  starting transfers between devices  117 us (15%)
  matrix products  103 us (13%)
  other arithmetic  73.3 us (10%)
  Pallas kernels  24.3 us (3%)
    ppermute x4, waiting for transfers between devices, gather_pieces(): outer = lax.ppermute(middle, 'dp', OUTWARD)  52.8 us
    convert_element_type x10, local copies, waits for them, and re-layouts, low(): return value.astype(jnp.bfloat16)  51.6 us
    unnamed x313, local copies, waits for them, and re-layouts  45.8 us
    ppermute x4, waiting for transfers between devices, reduce_group(): from_y = lax.ppermute(hop, 'dp', BESIDE)  32 us
    dynamic_slice x11, local copies, waits for them, and re-layouts, pick(): return lax.dynamic_index_in_dim(array, index, axis, keepdims=False)  31.9 us
    ppermute x4, starting transfers between devices, reduce_group(): other = lax.ppermute(total, 'stream', CORE)  28.6 us
    pallas_call x4, Pallas kernels, gather_group(): pl.pallas_call(functools.partial(assemble_kernel, units), out_shape=[jax....  24.3 us
    ppermute x4, waiting for transfers between devices, reduce_group(): first = lax.ppermute(hop, 'dp', INWARD)  22.9 us
  transfers between devices with their start and end apart: 88, of which 19 were waited for; matrix products, arithmetic and copies ran while one was open for 33% of the time, Pallas kernels for 3%

profile of v1, /device:TPU:1, one launch (start us, length us, event | category | flops | bytes accessed | tf_op | source)
XLA Modules:
  0.0 754.8 jit_solution(7276345646447521593)
XLA Ops:
  21.1 5.2 fusion.162
  59.8 8.9 %collective-permute-done.43 = bf16[2,2,192,384]{3,2,1,0:T(8,128)(2,1)S(1)} collective-permute-done((bf16[2,2,192,384]{3,2,1,0:T(8,128)(2,1)}, bf16[2,2,192,384]{3,2,1,0:T(8,128)(2,1)S(1)}, u32[]{:S(2)}, u32[]{:S(2)}) %collective-permute-start.43) | collective-permute-done | bytes 589856 | tf_op jit(solution)/shard_map/ppermute | solution.py:49
  75.0 33.7 %collective-permute-done.15 = bf16[2,2,224,384]{3,2,1,0:T(8,128)(2,1)S(1)} collective-permute-done((bf16[2,2,224,384]{3,2,1,0:T(8,128)(2,1)}, bf16[2,2,224,384]{3,2,1,0:T(8,128)(2,1)S(1)}, u32[]{:S(2)}, u32[]{:S(2)}) %collective-permute-start.15) | collective-permute-done | bytes 688160 | tf_op jit(solution)/shard_map/ppermute | solution.py:49
  112.4 3.0 collective-permute-done.6.refs_6_
  117.0 7.4 collective-permute-done.30
  129.5 7.2 assemble.4
  139.3 6.0 copy.331
  145.3 5.0 convolution_bitcast_fusion
  166.2 6.6 fusion.166
  176.0 5.5 assemble.5
  185.2 4.9 copy.341
  190.1 3.1 convolution_bitcast_fusion.1
  197.1 4.3 fusion.44
  223.3 5.4 assemble.7
  231.0 6.7 copy.358
  243.4 16.2 %collective-permute-done.33.refs_5_ = bf16[2,240,384]{2,1,0:T(8,128)(2,1)} collective-permute-done((bf16[2,240,384]{2,1,0:T(8,128)(2,1)}, bf16[2,240,384]{2,1,0:T(8,128)(2,1)}, u32[]{:S(2)}, u32[]{:S(2)}) %collective-permute-start.33) | collective-permute-done | bytes 368672 | tf_op jit(solution)/shard_map/ppermute | solution.py:54
  260.9 6.4 collective-permute-done.34.refs_6_
  269.7 3.1 fusion.53
  277.1 6.1 assemble.6
  288.9 6.8 copy.356
  299.7 4.1 gather_fusion.1
  314.3 16.7 %fusion.168 = (f32[8,12,40]{2,1,0:T(8,128)S(1)}, f32[8,12,40,145]{3,2,1,0:T(8,128)S(1)}) fusion(f32[8,12,40,145]{3,2,1,0:T(8,128)S(1)} %fusion.81), kind=kOutput, calls=%fused_computation.421 | output fusion | flops 2227344 | bytes 4469760 | tf_op jit(solution)/shard_map/sub | solution.py:254
  339.8 4.0 multiply_convert_fusion.2
  347.8 3.4 fusion.171
  358.7 5.1 multiply_reduce_fusion.1
  363.8 3.4 fusion.65
  377.0 4.6 convolution_convert_fusion.1
  381.6 4.5 convolution_convert_fusion
  386.1 3.7 broadcast_multiply_fusion
  390.9 4.8 bitcast_reduce_fusion
  402.8 6.3 copy.372
  412.3 9.6 %convert_element_type.908 = bf16[8,2,48,2,4,384]{5,4,3,2,1,0:T(4,128)(2,1)} reshape(bf16[768,3072]{1,0:T(8,128)(2,1)} %convolution_convert_fusion.1) | data formatting | bytes 9437184 | tf_op jit(solution)/shard_map/convert_element_type | solution.py:141
  422.0 5.4 copy.406
  427.4 10.3 %convert_element_type.947 = bf16[8,2,192,2,1,384]{5,3,2,1,0,4:T(2,128)(2,1)} reshape(bf16[3072,768]{1,0:T(8,128)(2,1)} %convolution_convert_fusion) | data formatting | bytes 9437184 | tf_op jit(solution)/shard_map/convert_element_type | solution.py:141
  441.2 10.0 %constant_dynamic-slice_fusion.11 = bf16[1,4,2,2,192,384]{5,0,4,3,2,1:T(2,128)(2,1)} fusion(bf16[2,4,2,2,192,384]{5,0,4,3,2,1:T(2,128)(2,1)} %bitcast.548, s32[]{:T(128)S(6)} %select_n.398), kind=kLoop, calls=%fused_computation.337 | loop fusion | bytes 4718596 | tf_op jit(solution)/shard_map/jit(dynamic_index_in_dim)/dynamic_slice | solution.py:24
  451.3 4.3 copy.517
  456.0 6.3 copy.371
  462.3 10.3 %fusion.7 = f32[4,2,2,145,768]{4,0,2,3,1:T(4,128)S(1)} fusion(f32[1,8,145,768]{3,1,2,0:T(8,128)} %copy.372, f32[1,8,145,768]{3,1,2,0:T(8,128)} %copy.371, pred[8,2]{0,1:T(4,128)(4,1)S(1)} %copy-done.117, pred[8,4]{0,1:T(4,128)(4,1)S(1)} %copy-done.116), kind=kOutput, calls=%fused_computation.25 | convolution fusion | flops 172830784 | bytes 14254128 | tf_op jit(solution)/shard_map/rim,jrpd->ijmpd/dot_general | solution.py:417
  472.6 2.9 copy-done.25
  475.5 3.0 slice.271
  485.3 5.7 constant_dynamic-slice_fusion.7
  496.1 3.9 convert_bitcast_fusion
  502.1 17.3 %collective-permute-done.54 = bf16[2,2,2,145,768]{4,0,2,3,1:T(2,128)(2,1)} collective-permute-done((bf16[2,2,2,145,768]{4,0,2,3,1:T(2,128)(2,1)}, bf16[2,2,2,145,768]{4,0,2,3,1:T(2,128)(2,1)}, u32[]{:S(2)}, u32[]{:S(2)}) %collective-permute-start.54) | collective-permute-done | bytes 1781792 | tf_op jit(solution)/shard_map/ppermute | solution.py:418
  519.4 3.7 slice_add_fusion
  537.1 4.3 copy.377
  541.4 3.2 convert_element_type.798
  554.8 3.5 fusion.14
  558.3 4.7 copy.391
  562.9 7.2 convert_element_type.850
  601.8 9.0 %collective-permute-done.82 = bf16[4,192,384]{2,1,0:T(8,128)(2,1)S(1)} collective-permute-done((bf16[4,192,384]{2,1,0:T(8,128)(2,1)S(1)}, bf16[4,192,384]{2,1,0:T(8,128)(2,1)S(1)}, u32[]{:S(2)}, u32[]{:S(2)}) %collective-permute-start.82) | collective-permute-done | bytes 589856 | tf_op jit(solution)/shard_map/ppermute | solution.py:155
  610.8 12.6 %collective-permute-done.74 = bf16[4,192,384]{2,1,0:T(8,128)(2,1)S(1)} collective-permute-done((bf16[4,192,384]{2,1,0:T(8,128)(2,1)S(1)}, bf16[4,192,384]{2,1,0:T(8,128)(2,1)S(1)}, u32[]{:S(2)}, u32[]{:S(2)}) %collective-permute-start.74) | collective-permute-done | bytes 589856 | tf_op jit(solution)/shard_map/ppermute | solution.py:155
  631.7 6.8 collective-permute-done.75
  641.1 10.1 %collective-permute-done.83 = bf16[2,2,192,384]{3,2,1,0:T(8,128)(2,1)S(1)} collective-permute-done((bf16[2,2,192,384]{3,2,1,0:T(8,128)(2,1)S(1)}, bf16[2,2,192,384]{3,2,1,0:T(8,128)(2,1)S(1)}, u32[]{:S(2)}, u32[]{:S(2)}) %collective-permute-start.83) | collective-permute-done | bytes 589856 | tf_op jit(solution)/shard_map/ppermute | solution.py:165
  652.9 4.8 collective-permute-start.77
  660.7 7.4 collective-permute-start.85
  671.8 4.4 collective-permute-done.66
  680.7 6.1 collective-permute-done.58
  689.7 4.1 collective-permute-start.79
  694.7 6.0 collective-permute-done.59
  701.6 8.0 %collective-permute-start.87 = (bf16[2,192,384]{2,1,0:T(8,128)(2,1)S(1)}, bf16[2,192,384]{2,1,0:T(8,128)(2,1)S(1)}, u32[]{:S(2)}, u32[]{:S(2)}) collective-permute-start(bf16[2,192,384]{2,1,0:T(8,128)(2,1)S(1)} %add_convert_fusion.8), channel_id=1, source_target_pairs={{0,1},{1,0},{2,3},{3,2},{4,5},{5,4},{6,7},{7,6},{8,9},{9,8},{10,11... | collective-permute-start | bytes 884744 | tf_op jit(solution)/shard_map/ppermute | solution.py:175
  709.8 5.2 collective-permute-start.61
  715.3 3.3 collective-permute-done.61
  719.7 3.4 collective-permute-done.69
  728.4 14.0 %collective-permute-start.63 = (bf16[2,160,384]{2,1,0:T(8,128)(2,1)S(1)}, bf16[2,160,384]{2,1,0:T(8,128)(2,1)S(1)}, u32[]{:S(2)}, u32[]{:S(2)}) collective-permute-start(bf16[2,160,384]{2,1,0:T(8,128)(2,1)S(1)} %add_convert_fusion.10), channel_id=1, source_target_pairs={{0,1},{1,0},{2,3},{3,2},{4,5},{5,4},{6,7},{7,6},{8,9},{9,8},{10,11... | collective-permute-start | bytes 737288 | tf_op jit(solution)/shard_map/ppermute | solution.py:175
  (736 shorter events, 318.5 us)
Async XLA Ops:
  4.7 33.8 %collective-permute-start.13 = (bf16[2,224,384]{2,1,0:T(8,128)(2,1)}, bf16[2,224,384]{2,1,0:T(8,128)(2,1)S(1)}, u32[]{:S(2)}, u32[]{:S(2)}) collective-permute-start(bf16[2,224,384]{2,1,0:T(8,128)(2,1)} %fusion.213), channel_id=1, source_target_pairs={{0,8},{8,0},{4,12},{12,4},{16,24},{24,16},{20,28},{28,20},{1,9},{9... | collective-permute-start | bytes 1032200 | tf_op jit(solution)/shard_map/ppermute | solution.py:46
  7.9 23.2 %collective-permute-start = (bf16[2,160,384]{2,1,0:T(8,128)(2,1)}, bf16[2,160,384]{2,1,0:T(8,128)(2,1)S(1)}, u32[]{:S(2)}, u32[]{:S(2)}) collective-permute-start(bf16[2,160,384]{2,1,0:T(8,128)(2,1)} %fusion.214), channel_id=1, source_target_pairs={{0,8},{8,0},{4,12},{12,4},{16,24},{24,16},{20,28},{28,20},{1,9},{9... | collective-permute-start | bytes 737288 | tf_op jit(solution)/shard_map/ppermute | solution.py:46
  12.9 19.7 %collective-permute-start.41 = (bf16[2,192,384]{2,1,0:T(8,128)(2,1)}, bf16[2,192,384]{2,1,0:T(8,128)(2,1)S(1)}, u32[]{:S(2)}, u32[]{:S(2)}) collective-permute-start(bf16[2,192,384]{2,1,0:T(8,128)(2,1)} %bitcast.455.clone.2), channel_id=1, source_target_pairs={{0,8},{8,0},{4,12},{12,4},{16,24},{24,16},{20,28},{28,20},{1,9},{9... | collective-permute-start | bytes 884744 | tf_op jit(solution)/shard_map/ppermute | solution.py:46
  18.9 17.1 %collective-permute-start.28 = (bf16[2,240,384]{2,1,0:T(8,128)(2,1)S(1)}, bf16[2,240,384]{2,1,0:T(8,128)(2,1)S(1)}, u32[]{:S(2)}, u32[]{:S(2)}) collective-permute-start(bf16[2,240,384]{2,1,0:T(8,128)(2,1)S(1)} %bitcast.611), channel_id=1, source_target_pairs={{0,8},{8,0},{4,12},{12,4},{16,24},{24,16},{20,28},{28,20},{1,9},{9... | collective-permute-start | bytes 1105928 | tf_op jit(solution)/shard_map/ppermute | solution.py:46
  34.6 15.1 %collective-permute-start.42 = (bf16[2,2,192,384]{3,2,1,0:T(8,128)(2,1)}, bf16[2,2,192,384]{3,2,1,0:T(8,128)(2,1)}, u32[]{:S(2)}, u32[]{:S(2)}) collective-permute-start(bf16[2,2,192,384]{3,2,1,0:T(8,128)(2,1)} %pad_maximum_fusion.10), channel_id=1, source_target_pairs={{8,16},{16,8},{12,20},{20,12},{9,17},{17,9},{13,21},{21,13},{10,18... | collective-permute-start | bytes 1769480 | tf_op jit(solution)/shard_map/ppermute | solution.py:48
  37.0 16.9 %collective-permute-start.29 = (bf16[2,2,240,384]{3,2,1,0:T(8,128)(2,1)}, bf16[2,2,240,384]{3,2,1,0:T(8,128)(2,1)}, u32[]{:S(2)}, u32[]{:S(2)}) collective-permute-start(bf16[2,2,240,384]{3,2,1,0:T(8,128)(2,1)} %pad_maximum_fusion.6), channel_id=1, source_target_pairs={{8,16},{16,8},{12,20},{20,12},{9,17},{17,9},{13,21},{21,13},{10,18... | collective-permute-start | bytes 2211848 | tf_op jit(solution)/shard_map/ppermute | solution.py:48
  41.8 16.1 %collective-permute-start.2 = (bf16[2,2,160,384]{3,2,1,0:T(8,128)(2,1)}, bf16[2,2,160,384]{3,2,1,0:T(8,128)(2,1)S(1)}, u32[]{:S(2)}, u32[]{:S(2)}) collective-permute-start(bf16[2,2,160,384]{3,2,1,0:T(8,128)(2,1)} %collective-permute-done.1), channel_id=1, source_target_pairs={{8,0},{12,4},{16,24},{20,28},{9,1},{13,5},{17,25},{21,29},{10,2},{... | collective-permute-start | bytes 1474568 | tf_op jit(solution)/shard_map/ppermute | solution.py:49
  46.5 24.3 %collective-permute-start.3 = (bf16[2,160,384]{2,1,0:T(8,128)(2,1)S(1)}, bf16[2,160,384]{2,1,0:T(8,128)(2,1)S(1)}, u32[]{:S(2)}, u32[]{:S(2)}) collective-permute-start(bf16[2,160,384]{2,1,0:T(8,128)(2,1)S(1)} %fusion.117), channel_id=1, source_target_pairs={{0,4},{4,0},{8,12},{12,8},{16,20},{20,16},{24,28},{28,24},{1,5},{5... | collective-permute-start | bytes 737288 | tf_op jit(solution)/shard_map/ppermute | solution.py:52
  49.6 19.1 %collective-permute-start.43 = (bf16[2,2,192,384]{3,2,1,0:T(8,128)(2,1)}, bf16[2,2,192,384]{3,2,1,0:T(8,128)(2,1)S(1)}, u32[]{:S(2)}, u32[]{:S(2)}) collective-permute-start(bf16[2,2,192,384]{3,2,1,0:T(8,128)(2,1)} %collective-permute-done.42), channel_id=1, source_target_pairs={{8,0},{12,4},{16,24},{20,28},{9,1},{13,5},{17,25},{21,29},{10,2},{... | collective-permute-start | bytes 1769480 | tf_op jit(solution)/shard_map/ppermute | solution.py:49
  51.8 58.2 %collective-permute-start.7 = (bf16[2,160,384]{2,1,0:T(8,128)(2,1)S(1)}, bf16[2,160,384]{2,1,0:T(8,128)(2,1)S(1)}, u32[]{:S(2)}, u32[]{:S(2)}) collective-permute-start(bf16[2,160,384]{2,1,0:T(8,128)(2,1)S(1)} %collective-permute-done.refs_1_), channel_id=1, source_target_pairs={{0,1},{1,0},{2,3},{3,2},{4,5},{5,4},{6,7},{7,6},{8,9},{9,8},{10,11... | collective-permute-start | bytes 737288 | tf_op jit(solution)/shard_map/ppermute | solution.py:57
  53.8 54.8 %collective-permute-start.15 = (bf16[2,2,224,384]{3,2,1,0:T(8,128)(2,1)}, bf16[2,2,224,384]{3,2,1,0:T(8,128)(2,1)S(1)}, u32[]{:S(2)}, u32[]{:S(2)}) collective-permute-start(bf16[2,2,224,384]{3,2,1,0:T(8,128)(2,1)} %collective-permute-done.14), channel_id=1, source_target_pairs={{8,0},{12,4},{16,24},{20,28},{9,1},{13,5},{17,25},{21,29},{10,2},{... | collective-permute-start | bytes 2064392 | tf_op jit(solution)/shard_map/ppermute | solution.py:49
  57.9 66.5 %collective-permute-start.30 = (bf16[2,2,240,384]{3,2,1,0:T(8,128)(2,1)}, bf16[2,2,240,384]{3,2,1,0:T(8,128)(2,1)S(1)}, u32[]{:S(2)}, u32[]{:S(2)}) collective-permute-start(bf16[2,2,240,384]{3,2,1,0:T(8,128)(2,1)} %collective-permute-done.29), channel_id=1, source_target_pairs={{8,0},{12,4},{16,24},{20,28},{9,1},{13,5},{17,25},{21,29},{10,2},{... | collective-permute-start | bytes 2211848 | tf_op jit(solution)/shard_map/ppermute | solution.py:49
  70.8 41.1 %collective-permute-start.16 = (bf16[2,224,384]{2,1,0:T(8,128)(2,1)S(1)}, bf16[2,224,384]{2,1,0:T(8,128)(2,1)}, u32[]{:S(2)}, u32[]{:S(2)}) collective-permute-start(bf16[2,224,384]{2,1,0:T(8,128)(2,1)S(1)} %fusion.110), channel_id=1, source_target_pairs={{0,4},{4,0},{8,12},{12,8},{16,20},{20,16},{24,28},{28,24},{1,5},{5... | collective-permute-start | bytes 1032200 | tf_op jit(solution)/shard_map/ppermute | solution.py:52
  73.8 38.1 %collective-permute-start.5 = (bf16[2,160,384]{2,1,0:T(8,128)(2,1)S(1)}, bf16[2,160,384]{2,1,0:T(8,128)(2,1)S(1)}, u32[]{:S(2)}, u32[]{:S(2)}) collective-permute-start(bf16[2,160,384]{2,1,0:T(8,128)(2,1)S(1)} %collective-permute-done.3.refs_3_), channel_id=1, source_target_pairs={{0,2},{2,0},{1,3},{3,1},{4,6},{6,4},{5,7},{7,5},{8,10},{10,8},{9,1... | collective-permute-start | bytes 737288 | tf_op jit(solution)/shard_map/ppermute | solution.py:54
  110.0 18.7 %collective-permute-start.8 = (bf16[2,2,160,384]{3,2,1,0:T(8,128)(2,1)S(1)}, bf16[2,2,160,384]{3,2,1,0:T(8,128)(2,1)S(1)}, u32[]{:S(2)}, u32[]{:S(2)}) collective-permute-start(bf16[2,2,160,384]{3,2,1,0:T(8,128)(2,1)S(1)} %broadcast_select_fusion.3.refs_2_), channel_id=1, source_target_pairs={{0,1},{1,0},{2,3},{3,2},{4,5},{5,4},{6,7},{7,6},{8,9},{9,8},{10,11... | collective-permute-start | bytes 1474568 | tf_op jit(solution)/shard_map/ppermute | solution.py:57
  111.9 14.1 %collective-permute-start.9 = (bf16[2,160,384]{2,1,0:T(8,128)(2,1)S(1)}, bf16[2,160,384]{2,1,0:T(8,128)(2,1)S(1)}, u32[]{:S(2)}, u32[]{:S(2)}) collective-permute-start(bf16[2,160,384]{2,1,0:T(8,128)(2,1)S(1)} %collective-permute-done.3.refs_3_), channel_id=1, source_target_pairs={{0,1},{1,0},{2,3},{3,2},{4,5},{5,4},{6,7},{7,6},{8,9},{9,8},{10,11... | collective-permute-start | bytes 737288 | tf_op jit(solution)/shard_map/ppermute | solution.py:57
  111.9 15.3 %collective-permute-start.11 = (bf16[2,160,384]{2,1,0:T(8,128)(2,1)S(1)}, bf16[2,160,384]{2,1,0:T(8,128)(2,1)S(1)}, u32[]{:S(2)}, u32[]{:S(2)}) collective-permute-start(bf16[2,160,384]{2,1,0:T(8,128)(2,1)S(1)} %collective-permute-done.5.refs_5_), channel_id=1, source_target_pairs={{0,1},{1,0},{2,3},{3,2},{4,5},{5,4},{6,7},{7,6},{8,9},{9,8},{10,11... | collective-permute-start | bytes 737288 | tf_op jit(solution)/shard_map/ppermute | solution.py:57
  126.0 39.0 %collective-permute-start.44 = (bf16[2,192,384]{2,1,0:T(8,128)(2,1)}, bf16[2,192,384]{2,1,0:T(8,128)(2,1)}, u32[]{:S(2)}, u32[]{:S(2)}) collective-permute-start(bf16[2,192,384]{2,1,0:T(8,128)(2,1)} %fusion.114), channel_id=1, source_target_pairs={{0,4},{4,0},{8,12},{12,8},{16,20},{20,16},{24,28},{28,24},{1,5},{5... | collective-permute-start | bytes 884744 | tf_op jit(solution)/shard_map/ppermute | solution.py:52
  127.2 38.5 %collective-permute-start.20 = (bf16[2,224,384]{2,1,0:T(8,128)(2,1)S(1)}, bf16[2,224,384]{2,1,0:T(8,128)(2,1)}, u32[]{:S(2)}, u32[]{:S(2)}) collective-permute-start(bf16[2,224,384]{2,1,0:T(8,128)(2,1)S(1)} %collective-permute-done.13.refs_1_), channel_id=1, source_target_pairs={{0,1},{1,0},{2,3},{3,2},{4,5},{5,4},{6,7},{7,6},{8,9},{9,8},{10,11... | collective-permute-start | bytes 1032200 | tf_op jit(solution)/shard_map/ppermute | solution.py:57
  127.5 38.1 %collective-permute-start.18 = (bf16[2,224,384]{2,1,0:T(8,128)(2,1)}, bf16[2,224,384]{2,1,0:T(8,128)(2,1)}, u32[]{:S(2)}, u32[]{:S(2)}) collective-permute-start(bf16[2,224,384]{2,1,0:T(8,128)(2,1)} %collective-permute-done.16.refs_3_), channel_id=1, source_target_pairs={{0,2},{2,0},{1,3},{3,1},{4,6},{6,4},{5,7},{7,5},{8,10},{10,8},{9,1... | collective-permute-start | bytes 1032200 | tf_op jit(solution)/shard_map/ppermute | solution.py:54
  128.7 47.0 %collective-permute-start.21 = (bf16[2,2,224,384]{3,2,1,0:T(8,128)(2,1)S(1)}, bf16[2,2,224,384]{3,2,1,0:T(8,128)(2,1)}, u32[]{:S(2)}, u32[]{:S(2)}) collective-permute-start(bf16[2,2,224,384]{3,2,1,0:T(8,128)(2,1)S(1)} %broadcast_select_fusion.1.refs_2_), channel_id=1, source_target_pairs={{0,1},{1,0},{2,3},{3,2},{4,5},{5,4},{6,7},{7,6},{8,9},{9,8},{10,11... | collective-permute-start | bytes 2064392 | tf_op jit(solution)/shard_map/ppermute | solution.py:57
  129.2 21.1 %collective-permute-start.17 = (bf16[2,224,384]{2,1,0:T(8,128)(2,1)}, bf16[2,224,384]{2,1,0:T(8,128)(2,1)}, u32[]{:S(2)}, u32[]{:S(2)}) collective-permute-start(bf16[2,224,384]{2,1,0:T(8,128)(2,1)} %dynamic-slice_bitcast_fusion.6), channel_id=1, source_target_pairs={{0,4},{4,0},{8,12},{12,8},{16,20},{20,16},{24,28},{28,24},{1,5},{5... | collective-permute-start | bytes 1032200 | tf_op jit(solution)/shard_map/ppermute | solution.py:53
  150.3 15.8 %collective-permute-start.19 = (bf16[2,224,384]{2,1,0:T(8,128)(2,1)}, bf16[2,224,384]{2,1,0:T(8,128)(2,1)}, u32[]{:S(2)}, u32[]{:S(2)}) collective-permute-start(bf16[2,224,384]{2,1,0:T(8,128)(2,1)} %collective-permute-done.17.refs_4_), channel_id=1, source_target_pairs={{0,2},{2,0},{1,3},{3,1},{4,6},{6,4},{5,7},{7,5},{8,10},{10,8},{9,1... | collective-permute-start | bytes 1032200 | tf_op jit(solution)/shard_map/ppermute | solution.py:55
  172.8 36.1 %collective-permute-start.48 = (bf16[2,192,384]{2,1,0:T(8,128)(2,1)}, bf16[2,192,384]{2,1,0:T(8,128)(2,1)}, u32[]{:S(2)}, u32[]{:S(2)}) collective-permute-start(bf16[2,192,384]{2,1,0:T(8,128)(2,1)} %copy-done.5), channel_id=1, source_target_pairs={{0,1},{1,0},{2,3},{3,2},{4,5},{5,4},{6,7},{7,6},{8,9},{9,8},{10,11... | collective-permute-start | bytes 884744 | tf_op jit(solution)/shard_map/ppermute | solution.py:57
  173.3 36.0 %collective-permute-start.31 = (bf16[2,240,384]{2,1,0:T(8,128)(2,1)}, bf16[2,240,384]{2,1,0:T(8,128)(2,1)}, u32[]{:S(2)}, u32[]{:S(2)}) collective-permute-start(bf16[2,240,384]{2,1,0:T(8,128)(2,1)} %fusion.108), channel_id=1, source_target_pairs={{0,4},{4,0},{8,12},{12,8},{16,20},{20,16},{24,28},{28,24},{1,5},{5... | collective-permute-start | bytes 1105928 | tf_op jit(solution)/shard_map/ppermute | solution.py:52
  174.5 28.1 %collective-permute-start.46 = (bf16[2,192,384]{2,1,0:T(8,128)(2,1)}, bf16[2,192,384]{2,1,0:T(8,128)(2,1)}, u32[]{:S(2)}, u32[]{:S(2)}) collective-permute-start(bf16[2,192,384]{2,1,0:T(8,128)(2,1)} %collective-permute-done.44.refs_3_), channel_id=1, source_target_pairs={{0,2},{2,0},{1,3},{3,1},{4,6},{6,4},{5,7},{7,5},{8,10},{10,8},{9,1... | collective-permute-start | bytes 884744 | tf_op jit(solution)/shard_map/ppermute | solution.py:54
  175.7 28.4 %collective-permute-start.45 = (bf16[2,192,384]{2,1,0:T(8,128)(2,1)}, bf16[2,192,384]{2,1,0:T(8,128)(2,1)}, u32[]{:S(2)}, u32[]{:S(2)}) collective-permute-start(bf16[2,192,384]{2,1,0:T(8,128)(2,1)} %dynamic-slice_bitcast_fusion.7), channel_id=1, source_target_pairs={{0,4},{4,0},{8,12},{12,8},{16,20},{20,16},{24,28},{28,24},{1,5},{5... | collective-permute-start | bytes 884744 | tf_op jit(solution)/shard_map/ppermute | solution.py:53
  209.4 86.3 %collective-permute-start.27 = (bf16[2,2,2,145,768]{4,2,3,1,0:T(2,128)(2,1)}, bf16[2,2,2,145,768]{4,2,3,1,0:T(2,128)(2,1)}, u32[]{:S(2)}, u32[]{:S(2)}) collective-permute-start(bf16[2,2,2,145,768]{4,2,3,1,0:T(2,128)(2,1)} %copy.346), channel_id=1, source_target_pairs={{0,2},{2,0},{1,3},{3,1},{4,6},{6,4},{5,7},{7,5},{8,10},{10,8},{9,1... | collective-permute-start | bytes 5345288 | tf_op jit(solution)/shard_map/ppermute | solution.py:321
  215.9 25.6 %collective-permute-start.35 = (bf16[2,240,384]{2,1,0:T(8,128)(2,1)S(1)}, bf16[2,240,384]{2,1,0:T(8,128)(2,1)}, u32[]{:S(2)}, u32[]{:S(2)}) collective-permute-start(bf16[2,240,384]{2,1,0:T(8,128)(2,1)S(1)} %collective-permute-done.28.refs_1_), channel_id=1, source_target_pairs={{0,1},{1,0},{2,3},{3,2},{4,5},{5,4},{6,7},{7,6},{8,9},{9,8},{10,11... | collective-permute-start | bytes 1105928 | tf_op jit(solution)/shard_map/ppermute | solution.py:57
  216.6 25.3 %collective-permute-start.32 = (bf16[2,240,384]{2,1,0:T(8,128)(2,1)}, bf16[2,240,384]{2,1,0:T(8,128)(2,1)}, u32[]{:S(2)}, u32[]{:S(2)}) collective-permute-start(bf16[2,240,384]{2,1,0:T(8,128)(2,1)} %dynamic-slice_bitcast_fusion.5), channel_id=1, source_target_pairs={{0,4},{4,0},{8,12},{12,8},{16,20},{20,16},{24,28},{28,24},{1,5},{5... | collective-permute-start | bytes 1105928 | tf_op jit(solution)/shard_map/ppermute | solution.py:53
  219.4 41.5 %collective-permute-start.37 = (bf16[2,240,384]{2,1,0:T(8,128)(2,1)}, bf16[2,240,384]{2,1,0:T(8,128)(2,1)}, u32[]{:S(2)}, u32[]{:S(2)}) collective-permute-start(bf16[2,240,384]{2,1,0:T(8,128)(2,1)} %collective-permute-done.31.refs_3_), channel_id=1, source_target_pairs={{0,1},{1,0},{2,3},{3,2},{4,5},{5,4},{6,7},{7,6},{8,9},{9,8},{10,11... | collective-permute-start | bytes 1105928 | tf_op jit(solution)/shard_map/ppermute | solution.py:57
  220.2 39.4 %collective-permute-start.33 = (bf16[2,240,384]{2,1,0:T(8,128)(2,1)}, bf16[2,240,384]{2,1,0:T(8,128)(2,1)}, u32[]{:S(2)}, u32[]{:S(2)}) collective-permute-start(bf16[2,240,384]{2,1,0:T(8,128)(2,1)} %collective-permute-done.31.refs_3_), channel_id=1, source_target_pairs={{0,2},{2,0},{1,3},{3,1},{4,6},{6,4},{5,7},{7,5},{8,10},{10,8},{9,1... | collective-permute-start | bytes 1105928 | tf_op jit(solution)/shard_map/ppermute | solution.py:54
  241.5 34.6 %collective-permute-start.36 = (bf16[2,2,240,384]{3,2,1,0:T(8,128)(2,1)S(1)}, bf16[2,2,240,384]{3,2,1,0:T(8,128)(2,1)}, u32[]{:S(2)}, u32[]{:S(2)}) collective-permute-start(bf16[2,2,240,384]{3,2,1,0:T(8,128)(2,1)S(1)} %broadcast_select_fusion.refs_2_), channel_id=1, source_target_pairs={{0,1},{1,0},{2,3},{3,2},{4,5},{5,4},{6,7},{7,6},{8,9},{9,8},{10,11... | collective-permute-start | bytes 2211848 | tf_op jit(solution)/shard_map/ppermute | solution.py:57
  241.9 25.4 %collective-permute-start.34 = (bf16[2,240,384]{2,1,0:T(8,128)(2,1)}, bf16[2,240,384]{2,1,0:T(8,128)(2,1)S(1)}, u32[]{:S(2)}, u32[]{:S(2)}) collective-permute-start(bf16[2,240,384]{2,1,0:T(8,128)(2,1)} %collective-permute-done.32.refs_4_), channel_id=1, source_target_pairs={{0,2},{2,0},{1,3},{3,1},{4,6},{6,4},{5,7},{7,5},{8,10},{10,8},{9,1... | collective-permute-start | bytes 1105928 | tf_op jit(solution)/shard_map/ppermute | solution.py:55
  259.6 15.8 %collective-permute-start.39 = (bf16[2,240,384]{2,1,0:T(8,128)(2,1)}, bf16[2,240,384]{2,1,0:T(8,128)(2,1)S(1)}, u32[]{:S(2)}, u32[]{:S(2)}) collective-permute-start(bf16[2,240,384]{2,1,0:T(8,128)(2,1)} %collective-permute-done.33.refs_5_), channel_id=1, source_target_pairs={{0,1},{1,0},{2,3},{3,2},{4,5},{5,4},{6,7},{7,6},{8,9},{9,8},{10,11... | collective-permute-start | bytes 1105928 | tf_op jit(solution)/shard_map/ppermute | solution.py:57
  260.9 15.2 %collective-permute-start.38 = (bf16[2,240,384]{2,1,0:T(8,128)(2,1)}, bf16[2,240,384]{2,1,0:T(8,128)(2,1)}, u32[]{:S(2)}, u32[]{:S(2)}) collective-permute-start(bf16[2,240,384]{2,1,0:T(8,128)(2,1)} %collective-permute-done.32.refs_4_), channel_id=1, source_target_pairs={{0,1},{1,0},{2,3},{3,2},{4,5},{5,4},{6,7},{7,6},{8,9},{9,8},{10,11... | collective-permute-start | bytes 1105928 | tf_op jit(solution)/shard_map/ppermute | solution.py:57
  455.5 93.5 %collective-permute-start.80 = (bf16[4,2,2,192,384]{4,3,2,0,1:T(8,128)(2,1)}, bf16[4,2,2,192,384]{4,3,2,0,1:T(8,128)(2,1)}, u32[]{:S(2)}, u32[]{:S(2)}) collective-permute-start(bf16[4,2,2,192,384]{4,3,2,0,1:T(8,128)(2,1)} %bitcast.521), channel_id=1, source_target_pairs={{0,1},{1,0},{2,3},{3,2},{4,5},{5,4},{6,7},{7,6},{8,9},{9,8},{10,11... | collective-permute-start | bytes 7077896 | tf_op jit(solution)/shard_map/ppermute | solution.py:150
  455.5 124.0 %collective-permute-start.72 = (bf16[4,2,2,192,384]{4,3,0,2,1:T(8,128)(2,1)}, bf16[4,2,2,192,384]{4,3,0,2,1:T(8,128)(2,1)}, u32[]{:S(2)}, u32[]{:S(2)}) collective-permute-start(bf16[4,2,2,192,384]{4,3,0,2,1:T(8,128)(2,1)} %copy.407), channel_id=1, source_target_pairs={{0,1},{1,0},{2,3},{3,2},{4,5},{5,4},{6,7},{7,6},{8,9},{9,8},{10,11... | collective-permute-start | bytes 7077896 | tf_op jit(solution)/shard_map/ppermute | solution.py:150
  478.6 40.8 %collective-permute-start.54 = (bf16[2,2,2,145,768]{4,0,2,3,1:T(2,128)(2,1)}, bf16[2,2,2,145,768]{4,0,2,3,1:T(2,128)(2,1)}, u32[]{:S(2)}, u32[]{:S(2)}) collective-permute-start(bf16[2,2,2,145,768]{4,0,2,3,1:T(2,128)(2,1)} %slice.271), channel_id=1, source_target_pairs={{0,2},{2,0},{1,3},{3,1},{4,6},{6,4},{5,7},{7,5},{8,10},{10,8},{9,1... | collective-permute-start | bytes 5345288 | tf_op jit(solution)/shard_map/ppermute | solution.py:418
  526.7 24.6 %collective-permute-start.55 = (bf16[2,2,145,768]{3,1,2,0:T(2,128)(2,1)}, bf16[2,2,145,768]{3,1,2,0:T(2,128)(2,1)}, u32[]{:S(2)}, u32[]{:S(2)}) collective-permute-start(bf16[2,2,145,768]{3,1,2,0:T(2,128)(2,1)} %copy.374), channel_id=1, source_target_pairs={{0,1},{1,0},{2,3},{3,2},{4,5},{5,4},{6,7},{7,6},{8,9},{9,8},{10,11... | collective-permute-start | bytes 2672648 | tf_op jit(solution)/shard_map/ppermute | solution.py:420
  551.1 43.3 %collective-permute-start.81 = (bf16[4,192,384]{2,1,0:T(8,128)(2,1)}, bf16[4,192,384]{2,1,0:T(8,128)(2,1)}, u32[]{:S(2)}, u32[]{:S(2)}) collective-permute-start(bf16[4,192,384]{2,1,0:T(8,128)(2,1)} %fusion.55), channel_id=1, source_target_pairs={{0,2},{2,0},{1,3},{3,1},{4,6},{6,4},{5,7},{7,5},{8,10},{10,8},{9,1... | collective-permute-start | bytes 1769480 | tf_op jit(solution)/shard_map/ppermute | solution.py:153
  579.2 50.7 %collective-permute-start.64 = (bf16[4,2,2,272,384]{4,3,0,2,1:T(8,128)(2,1)}, bf16[4,2,2,272,384]{4,3,0,2,1:T(8,128)(2,1)}, u32[]{:S(2)}, u32[]{:S(2)}) collective-permute-start(bf16[4,2,2,272,384]{4,3,0,2,1:T(8,128)(2,1)} %copy.399), channel_id=1, source_target_pairs={{0,1},{1,0},{2,3},{3,2},{4,5},{5,4},{6,7},{7,6},{8,9},{9,8},{10,11... | collective-permute-start | bytes 10027016 | tf_op jit(solution)/shard_map/ppermute | solution.py:150
  581.7 15.9 %collective-permute-start.73 = (bf16[4,192,384]{2,1,0:T(8,128)(2,1)}, bf16[4,192,384]{2,1,0:T(8,128)(2,1)}, u32[]{:S(2)}, u32[]{:S(2)}) collective-permute-start(bf16[4,192,384]{2,1,0:T(8,128)(2,1)} %fusion.58), channel_id=1, source_target_pairs={{0,2},{2,0},{1,3},{3,1},{4,6},{6,4},{5,7},{7,5},{8,10},{10,8},{9,1... | collective-permute-start | bytes 1769480 | tf_op jit(solution)/shard_map/ppermute | solution.py:153
  596.3 14.4 %collective-permute-start.82 = (bf16[4,192,384]{2,1,0:T(8,128)(2,1)S(1)}, bf16[4,192,384]{2,1,0:T(8,128)(2,1)S(1)}, u32[]{:S(2)}, u32[]{:S(2)}) collective-permute-start(bf16[4,192,384]{2,1,0:T(8,128)(2,1)S(1)} %fusion.57), channel_id=1, source_target_pairs={{0,4},{4,0},{8,12},{12,8},{16,20},{20,16},{24,28},{28,24},{1,5},{5... | collective-permute-start | bytes 1769480 | tf_op jit(solution)/shard_map/ppermute | solution.py:155
  599.2 24.1 %collective-permute-start.74 = (bf16[4,192,384]{2,1,0:T(8,128)(2,1)S(1)}, bf16[4,192,384]{2,1,0:T(8,128)(2,1)S(1)}, u32[]{:S(2)}, u32[]{:S(2)}) collective-permute-start(bf16[4,192,384]{2,1,0:T(8,128)(2,1)S(1)} %fusion.60), channel_id=1, source_target_pairs={{0,4},{4,0},{8,12},{12,8},{16,20},{20,16},{24,28},{28,24},{1,5},{5... | collective-permute-start | bytes 1769480 | tf_op jit(solution)/shard_map/ppermute | solution.py:155
  600.4 51.9 %collective-permute-start.56 = (bf16[4,2,2,160,384]{4,3,0,2,1:T(8,128)(2,1)S(1)}, bf16[4,2,2,160,384]{4,3,0,2,1:T(8,128)(2,1)S(1)}, u32[]{:S(2)}, u32[]{:S(2)}) collective-permute-start(bf16[4,2,2,160,384]{4,3,0,2,1:T(8,128)(2,1)S(1)} %copy.381), channel_id=1, source_target_pairs={{0,1},{1,0},{2,3},{3,2},{4,5},{5,4},{6,7},{7,6},{8,9},{9,8},{10,11... | collective-permute-start | bytes 5898248 | tf_op jit(solution)/shard_map/ppermute | solution.py:150
  624.6 13.9 %collective-permute-start.75 = (bf16[2,2,192,384]{3,2,1,0:T(8,128)(2,1)S(1)}, bf16[2,2,192,384]{3,2,1,0:T(8,128)(2,1)S(1)}, u32[]{:S(2)}, u32[]{:S(2)}) collective-permute-start(bf16[2,2,192,384]{3,2,1,0:T(8,128)(2,1)S(1)} %dynamic-slice_bitcast_fusion.4), channel_id=1, source_target_pairs={{0,8},{4,12},{24,16},{28,20},{1,9},{5,13},{25,17},{29,21},{2,10},{... | collective-permute-start | bytes 1769480 | tf_op jit(solution)/shard_map/ppermute | solution.py:165
  628.6 22.6 %collective-permute-start.83 = (bf16[2,2,192,384]{3,2,1,0:T(8,128)(2,1)S(1)}, bf16[2,2,192,384]{3,2,1,0:T(8,128)(2,1)S(1)}, u32[]{:S(2)}, u32[]{:S(2)}) collective-permute-start(bf16[2,2,192,384]{3,2,1,0:T(8,128)(2,1)S(1)} %dynamic-slice_bitcast_fusion.3), channel_id=1, source_target_pairs={{0,8},{4,12},{24,16},{28,20},{1,9},{5,13},{25,17},{29,21},{2,10},{... | collective-permute-start | bytes 1769480 | tf_op jit(solution)/shard_map/ppermute | solution.py:165
  631.3 26.4 %collective-permute-start.65 = (bf16[4,272,384]{2,1,0:T(8,128)(2,1)S(1)}, bf16[4,272,384]{2,1,0:T(8,128)(2,1)S(1)}, u32[]{:S(2)}, u32[]{:S(2)}) collective-permute-start(bf16[4,272,384]{2,1,0:T(8,128)(2,1)S(1)} %fusion.30), channel_id=1, source_target_pairs={{0,2},{2,0},{1,3},{3,1},{4,6},{6,4},{5,7},{7,5},{8,10},{10,8},{9,1... | collective-permute-start | bytes 2506760 | tf_op jit(solution)/shard_map/ppermute | solution.py:153
  638.7 14.2 %collective-permute-start.76 = (bf16[2,2,192,384]{3,2,1,0:T(8,128)(2,1)S(1)}, bf16[2,2,192,384]{3,2,1,0:T(8,128)(2,1)S(1)}, u32[]{:S(2)}, u32[]{:S(2)}) collective-permute-start(bf16[2,2,192,384]{3,2,1,0:T(8,128)(2,1)S(1)} %add_convert_fusion.2), channel_id=1, source_target_pairs={{8,16},{16,8},{12,20},{20,12},{9,17},{17,9},{13,21},{21,13},{10,18... | collective-permute-start | bytes 1769480 | tf_op jit(solution)/shard_map/ppermute | solution.py:166
  652.4 16.3 %collective-permute-start.57 = (bf16[4,160,384]{2,1,0:T(8,128)(2,1)S(1)}, bf16[4,160,384]{2,1,0:T(8,128)(2,1)S(1)}, u32[]{:S(2)}, u32[]{:S(2)}) collective-permute-start(bf16[4,160,384]{2,1,0:T(8,128)(2,1)S(1)} %fusion.62), channel_id=1, source_target_pairs={{0,2},{2,0},{1,3},{3,1},{4,6},{6,4},{5,7},{7,5},{8,10},{10,8},{9,1... | collective-permute-start | bytes 1474568 | tf_op jit(solution)/shard_map/ppermute | solution.py:153
  652.9 15.2 %collective-permute-start.77 = (bf16[2,192,384]{2,1,0:T(8,128)(2,1)S(1)}, bf16[2,192,384]{2,1,0:T(8,128)(2,1)S(1)}, u32[]{:S(2)}, u32[]{:S(2)}) collective-permute-start(bf16[2,192,384]{2,1,0:T(8,128)(2,1)S(1)} %fusion.88), channel_id=1, source_target_pairs={{0,8},{8,0},{4,12},{12,4},{16,24},{24,16},{20,28},{28,20},{1,9},{9... | collective-permute-start | bytes 884744 | tf_op jit(solution)/shard_map/ppermute | solution.py:170
  659.2 17.1 %collective-permute-start.66 = (bf16[4,272,384]{2,1,0:T(8,128)(2,1)S(1)}, bf16[4,272,384]{2,1,0:T(8,128)(2,1)S(1)}, u32[]{:S(2)}, u32[]{:S(2)}) collective-permute-start(bf16[4,272,384]{2,1,0:T(8,128)(2,1)S(1)} %fusion.32), channel_id=1, source_target_pairs={{0,4},{4,0},{8,12},{12,8},{16,20},{20,16},{24,28},{28,24},{1,5},{5... | collective-permute-start | bytes 2506760 | tf_op jit(solution)/shard_map/ppermute | solution.py:155
  660.7 18.7 %collective-permute-start.85 = (bf16[2,192,384]{2,1,0:T(8,128)(2,1)S(1)}, bf16[2,192,384]{2,1,0:T(8,128)(2,1)S(1)}, u32[]{:S(2)}, u32[]{:S(2)}) collective-permute-start(bf16[2,192,384]{2,1,0:T(8,128)(2,1)S(1)} %fusion.85), channel_id=1, source_target_pairs={{0,8},{8,0},{4,12},{12,4},{16,24},{24,16},{20,28},{28,20},{1,9},{9... | collective-permute-start | bytes 884744 | tf_op jit(solution)/shard_map/ppermute | solution.py:170
  668.2 21.4 %collective-permute-start.78 = (bf16[2,192,384]{2,1,0:T(8,128)(2,1)S(1)}, bf16[2,192,384]{2,1,0:T(8,128)(2,1)S(1)}, u32[]{:S(2)}, u32[]{:S(2)}) collective-permute-start(bf16[2,192,384]{2,1,0:T(8,128)(2,1)S(1)} %fusion.90), channel_id=1, source_target_pairs={{0,2},{2,0},{1,3},{3,1},{4,6},{6,4},{5,7},{7,5},{8,10},{10,8},{9,1... | collective-permute-start | bytes 884744 | tf_op jit(solution)/shard_map/ppermute | solution.py:172
  668.9 17.9 %collective-permute-start.58 = (bf16[4,160,384]{2,1,0:T(8,128)(2,1)S(1)}, bf16[4,160,384]{2,1,0:T(8,128)(2,1)S(1)}, u32[]{:S(2)}, u32[]{:S(2)}) collective-permute-start(bf16[4,160,384]{2,1,0:T(8,128)(2,1)S(1)} %fusion.64), channel_id=1, source_target_pairs={{0,4},{4,0},{8,12},{12,8},{16,20},{20,16},{24,28},{28,24},{1,5},{5... | collective-permute-start | bytes 1474568 | tf_op jit(solution)/shard_map/ppermute | solution.py:155
  677.1 16.6 %collective-permute-start.67 = (bf16[2,2,272,384]{3,2,1,0:T(8,128)(2,1)S(1)}, bf16[2,2,272,384]{3,2,1,0:T(8,128)(2,1)S(1)}, u32[]{:S(2)}, u32[]{:S(2)}) collective-permute-start(bf16[2,2,272,384]{3,2,1,0:T(8,128)(2,1)S(1)} %dynamic-slice_bitcast_fusion.2), channel_id=1, source_target_pairs={{0,8},{4,12},{24,16},{28,20},{1,9},{5,13},{25,17},{29,21},{2,10},{... | collective-permute-start | bytes 2506760 | tf_op jit(solution)/shard_map/ppermute | solution.py:165
  679.6 22.0 %collective-permute-start.86 = (bf16[2,192,384]{2,1,0:T(8,128)(2,1)S(1)}, bf16[2,192,384]{2,1,0:T(8,128)(2,1)S(1)}, u32[]{:S(2)}, u32[]{:S(2)}) collective-permute-start(bf16[2,192,384]{2,1,0:T(8,128)(2,1)S(1)} %fusion.87), channel_id=1, source_target_pairs={{0,2},{2,0},{1,3},{3,1},{4,6},{6,4},{5,7},{7,5},{8,10},{10,8},{9,1... | collective-permute-start | bytes 884744 | tf_op jit(solution)/shard_map/ppermute | solution.py:172
  687.3 13.4 %collective-permute-start.59 = (bf16[2,2,160,384]{3,2,1,0:T(8,128)(2,1)S(1)}, bf16[2,2,160,384]{3,2,1,0:T(8,128)(2,1)S(1)}, u32[]{:S(2)}, u32[]{:S(2)}) collective-permute-start(bf16[2,2,160,384]{3,2,1,0:T(8,128)(2,1)S(1)} %copy_bitcast_fusion.7), channel_id=1, source_target_pairs={{0,8},{4,12},{24,16},{28,20},{1,9},{5,13},{25,17},{29,21},{2,10},{... | collective-permute-start | bytes 1474568 | tf_op jit(solution)/shard_map/ppermute | solution.py:165
  689.7 20.0 %collective-permute-start.79 = (bf16[2,192,384]{2,1,0:T(8,128)(2,1)S(1)}, bf16[2,192,384]{2,1,0:T(8,128)(2,1)S(1)}, u32[]{:S(2)}, u32[]{:S(2)}) collective-permute-start(bf16[2,192,384]{2,1,0:T(8,128)(2,1)S(1)} %add_convert_fusion.9), channel_id=1, source_target_pairs={{0,1},{1,0},{2,3},{3,2},{4,5},{5,4},{6,7},{7,6},{8,9},{9,8},{10,11... | collective-permute-start | bytes 884744 | tf_op jit(solution)/shard_map/ppermute | solution.py:175
  694.0 21.0 %collective-permute-start.68 = (bf16[2,2,272,384]{3,2,1,0:T(8,128)(2,1)S(1)}, bf16[2,2,272,384]{3,2,1,0:T(8,128)(2,1)S(1)}, u32[]{:S(2)}, u32[]{:S(2)}) collective-permute-start(bf16[2,2,272,384]{3,2,1,0:T(8,128)(2,1)S(1)} %add_convert_fusion), channel_id=1, source_target_pairs={{8,16},{16,8},{12,20},{20,12},{9,17},{17,9},{13,21},{21,13},{10,18... | collective-permute-start | bytes 2506760 | tf_op jit(solution)/shard_map/ppermute | solution.py:166
  701.6 13.6 %collective-permute-start.87 = (bf16[2,192,384]{2,1,0:T(8,128)(2,1)S(1)}, bf16[2,192,384]{2,1,0:T(8,128)(2,1)S(1)}, u32[]{:S(2)}, u32[]{:S(2)}) collective-permute-start(bf16[2,192,384]{2,1,0:T(8,128)(2,1)S(1)} %add_convert_fusion.8), channel_id=1, source_target_pairs={{0,1},{1,0},{2,3},{3,2},{4,5},{5,4},{6,7},{7,6},{8,9},{9,8},{10,11... | collective-permute-start | bytes 884744 | tf_op jit(solution)/shard_map/ppermute | solution.py:175
  723.2 19.2 %collective-permute-start.70 = (bf16[2,272,384]{2,1,0:T(8,128)(2,1)S(1)}, bf16[2,272,384]{2,1,0:T(8,128)(2,1)S(1)}, u32[]{:S(2)}, u32[]{:S(2)}) collective-permute-start(bf16[2,272,384]{2,1,0:T(8,128)(2,1)S(1)} %fusion.76), channel_id=1, source_target_pairs={{0,2},{2,0},{1,3},{3,1},{4,6},{6,4},{5,7},{7,5},{8,10},{10,8},{9,1... | collective-permute-start | bytes 1253384 | tf_op jit(solution)/shard_map/ppermute | solution.py:172
  728.4 16.6 %collective-permute-start.63 = (bf16[2,160,384]{2,1,0:T(8,128)(2,1)S(1)}, bf16[2,160,384]{2,1,0:T(8,128)(2,1)S(1)}, u32[]{:S(2)}, u32[]{:S(2)}) collective-permute-start(bf16[2,160,384]{2,1,0:T(8,128)(2,1)S(1)} %add_convert_fusion.10), channel_id=1, source_target_pairs={{0,1},{1,0},{2,3},{3,2},{4,5},{5,4},{6,7},{7,6},{8,9},{9,8},{10,11... | collective-permute-start | bytes 737288 | tf_op jit(solution)/shard_map/ppermute | solution.py:175
  (172 other events, 1272.7 us)
